TPU v7x, 256 devices: a whole 4x4x8 slice. The times are simulated.
256 devices in a mesh: dom: 16 (over x, y), tp: 16 (over z, core).
Axes of the slice: x: 4, y: 4, z: 8, core: 2. Of those that a mesh axis runs over, the one named last changes fastest.
Arguments:
- latent: bfloat16 [1024, 65536], P('tp', 'dom'), may hold values from -6 to 6
- w_first: bfloat16 [1024, 1024], P(None, 'tp'), may hold values from -0.1875 to 0.1875
- w_second: bfloat16 [1024, 1024], P('tp'), may hold values from -0.1875 to 0.1875
- w_env: bfloat16 [1024, 256], P('tp'), may hold values from -0.1875 to 0.1875
- edge_vec: float32 [3, 65536], P(None, 'dom'), may hold values from -3 to 3, as said below
- centers: int32 [65536], P('dom'), may hold values from 0 to 127
- block_dest: int32 [512, 1], P('dom'), may hold values from 0 to 15; in each aligned block of 32 rows (0 to 31, 32 to 63, ...) at most 4 rows name the same one
- block_fill: int32 [512], P('dom'), may hold values from 64 to 128
- species: int32 [2048], P('dom'), may hold values from 0 to 3
- species_gain: float32 [4, 256], P(None, 'tp'), may hold values from 0.1 to 1.9
Outputs:
- latent_new: bfloat16 [1024, 65536], P('tp', 'dom')
- env_out: float32 [9, 256, 2048], P(None, 'tp', 'dom')
- invariants: float32 [3, 256, 65536], P(None, 'tp', 'dom')
Inputs may be any that keep to these rules, and one draw needn't show every extreme that they name: `block_dest`: in the 32 blocks of one domain no destination domain is named more than 4 times, a bound that some block reaches. `edge_vec`: every component has magnitude 0.5 to 3.
All inputs are finite; a program needn't handle non-finite values.
Results may differ from a plain program's by a relative error of at most 0.0077.
Values may be sent and summed in bfloat16 or wider, within the bound.
A program may use at most 128 MiB of HBM per device.

v0:
```python
import math

import jax
import jax.numpy as jnp
from jax import lax
from jax.sharding import PartitionSpec as P

root_three = math.sqrt(3.0)
root_five = math.sqrt(5.0)
root_fifteen = math.sqrt(15.0)
cutoff_radius = 6.0
env_factor = 0.25


def harmonics(vectors):
    along_x = vectors[0]
    along_y = vectors[1]
    along_z = vectors[2]
    radius = jnp.sqrt(along_x * along_x + along_y * along_y + along_z * along_z)
    unit_x = along_x / radius
    unit_y = along_y / radius
    unit_z = along_z / radius
    ratio = radius / cutoff_radius
    envelope = (1.0 - ratio * ratio) ** 2
    parts = [
        jnp.ones_like(unit_x),
        root_three * unit_x,
        root_three * unit_y,
        root_three * unit_z,
        root_fifteen * unit_x * unit_y,
        root_fifteen * unit_y * unit_z,
        root_five / 2.0 * (3.0 * unit_z * unit_z - 1.0),
        root_fifteen * unit_x * unit_z,
        root_fifteen / 2.0 * (unit_x * unit_x - unit_y * unit_y),
    ]
    return jnp.stack(parts) * envelope[None, :]


def contract_rows(left, right):
    return lax.dot_general(
        left, right, (((0,), (0,)), ((), ())), preferred_element_type=jnp.float32
    )


def on_device(
    latent,
    w_first,
    w_second,
    w_env,
    edge_vec,
    centers,
    block_dest,
    block_fill,
    species,
    species_gain,
):
    domains = lax.axis_size("dom")
    nblocks = block_fill.shape[0]
    slots = max(2, 2 * nblocks // domains)
    chan_local = species_gain.shape[1]
    pre_act = contract_rows(w_first, lax.all_gather(latent, "tp", axis=0, tiled=True))
    hidden = jax.nn.silu(pre_act).astype(jnp.bfloat16)
    columns = w_second
    update = lax.psum_scatter(contract_rows(columns, hidden), "tp", scatter_dimension=0, tiled=True)
    latent_new = (latent.astype(jnp.float32) + update).astype(jnp.bfloat16)
    columns = w_env
    weights = lax.psum_scatter(
        contract_rows(columns, latent_new), "tp", scatter_dimension=0, tiled=True
    ).astype(jnp.bfloat16)
    harmonic = harmonics(edge_vec)
    harmonic_blocks = harmonic.reshape(9, nblocks, 128).transpose(1, 0, 2)[:, :, None, :]
    weight_blocks = (
        weights.astype(jnp.float32)
        .reshape(chan_local, nblocks, 128)
        .transpose(1, 0, 2)[:, None, :, :]
    )
    slot_pos = jnp.arange(128, dtype=jnp.int32)[None, :]
    alive_mask = (slot_pos < block_fill[:, None]).astype(jnp.float32)[:, None, None, :]
    contrib = (harmonic_blocks * weight_blocks * alive_mask).astype(jnp.bfloat16)
    target = block_dest[:, 0]
    block_order = jnp.arange(nblocks, dtype=jnp.int32)
    earlier = (target[:, None] == target[None, :]) & (block_order[None, :] < block_order[:, None])
    slot_rank = jnp.sum(earlier.astype(jnp.int32), axis=1)
    position = target * slots + slot_rank
    outgoing = (
        jnp.zeros((domains * slots, 9, chan_local, 128), jnp.bfloat16).at[position].set(contrib)
    )
    center_blocks = centers.reshape(nblocks, 128)
    outgoing_idx = jnp.zeros((domains * slots, 128), jnp.int32).at[position].set(center_blocks)
    incoming = lax.all_to_all(outgoing, "dom", split_axis=0, concat_axis=0, tiled=True)
    incoming_idx = lax.all_to_all(outgoing_idx, "dom", split_axis=0, concat_axis=0, tiled=True)
    atoms_local = species.shape[0]
    flattened = incoming.astype(jnp.float32).transpose(0, 3, 1, 2).reshape(-1, 9 * chan_local)
    summed = jax.ops.segment_sum(flattened, incoming_idx.reshape(-1), num_segments=atoms_local)
    env_raw = summed.T.reshape(9, chan_local, atoms_local)
    species_ids = jnp.arange(species_gain.shape[0], dtype=jnp.int32)
    gain_sel = jnp.sum(
        jnp.where(
            species[None, :, None] == species_ids[:, None, None], species_gain[:, None, :], 0.0
        ),
        axis=0,
    )
    env_out = env_raw * gain_sel.T[None, :, :] * env_factor
    env_half = env_out.astype(jnp.bfloat16)
    looked = jnp.take(env_half, incoming_idx, axis=2).transpose(2, 0, 1, 3)
    returned = lax.all_to_all(looked, "dom", split_axis=0, concat_axis=0, tiled=True)
    own_env = returned[position]
    products = own_env.astype(jnp.float32) * harmonic_blocks
    degree_sums = jnp.stack(
        [products[:, 0], jnp.sum(products[:, 1:4], axis=1), jnp.sum(products[:, 4:9], axis=1)],
        axis=1,
    )
    invariants = degree_sums * weight_blocks * alive_mask
    invariants = invariants.transpose(1, 2, 0, 3).reshape(3, chan_local, nblocks * 128)
    return (latent_new, env_out, invariants)


def solution(mesh):
    in_specs = (
        P("tp", "dom"),
        P(None, "tp"),
        P("tp", None),
        P("tp", None),
        P(None, "dom"),
        P("dom"),
        P("dom", None),
        P("dom"),
        P("dom"),
        P(None, "tp"),
    )
    out_specs = (P("tp", "dom"), P(None, "tp", "dom"), P(None, "tp", "dom"))
    return jax.shard_map(
        on_device, mesh=mesh, in_specs=in_specs, out_specs=out_specs, check_vma=False
    )
```

profile of v0, /device:TPU:8, one launch (start us, length us, event | category | flops | bytes accessed | tf_op | source)
XLA Modules:
  0.0 523.2 jit_solution(16141304577326815327)
XLA Ops:
  7.2 0.0 copy-start
  7.2 0.0 all-gather.2.cloned.1.call-start
  7.2 0.7 all-gather.2.cloned.1.call-update
  7.9 0.0 reduce-scatter.7.cloned.1.call-start
  8.0 60.7 %all-gather.2.cloned.1.call-done = bf16[1024,4096]{1,0:T(8,128)(2,1)} async-done(((bf16[64,4096]{1,0:T(8,128)(2,1)}), bf16[1024,4096]{1,0:T(8,128)(2,1)}) %all-gather.2.cloned.1.call-update) | async-done | bytes 8388624 | tf_op jit(solution)/shard_map/all_gather | solution.py:61
  68.7 12.1 %convolution_bitcast_fusion = f32[1024,4096]{0,1:T(8,128)} fusion(bf16[64,1024]{1,0:T(8,128)(2,1)S(1)} %copy-done, bf16[1024,64]{0,1:T(8,128)(2,1)} %param.11, bf16[1024,4096]{1,0:T(8,128)(2,1)} %all-gather.2.cloned.1.call-done), kind=kOutput, calls=%fused_computation.5 | convolution fusion | flops 1075052544 | bytes 25427968 | tf_op jit(solution)/shard_map/dot_general | solution.py:40
  80.8 17.5 %copy.87 = f32[1024,4096]{1,0:T(8,128)} copy(f32[1024,4096]{0,1:T(8,128)} %convolution_bitcast_fusion) | data formatting | bytes 33554432
  98.3 0.0 reduce-scatter.7.cloned.1.call-update
  98.3 0.0 reduce-scatter.9.cloned.1.call-start
  98.4 1.0 copy-done.6
  99.3 1.3 copy.68
  100.7 96.9 %reduce-scatter.7.cloned.1.call-done = f32[64,4096]{1,0:T(8,128)} async-done(((f32[1024,4096]{1,0:T(8,128)}), f32[64,4096]{1,0:T(8,128)}) %reduce-scatter.7.cloned.1.call-update) | async-done | bytes 1048592
  197.5 1.8 copy.88
  199.4 0.0 copy-start.11
  199.4 1.4 add_convert_fusion
  200.8 2.6 convolution_bitcast_fusion.1
  203.5 5.6 %copy.89 = f32[256,4096]{1,0:T(8,128)} copy(f32[256,4096]{0,1:T(8,128)} %convolution_bitcast_fusion.1) | data formatting | bytes 8388608
  209.1 0.0 reduce-scatter.9.cloned.1.call-update
  209.1 0.6 copy-done.18
  209.7 0.2 convert_reduce_fusion
  209.9 1.2 scatter_custom_fusion
  211.2 7.3 %all-to-all-start = ((s32[16,4,128]{2,1,0:T(4,128)}), s32[16,4,128]{2,1,0:T(4,128)S(1)}, u32[]{:S(2)}, u32[]{:S(2)}) async-start(s32[16,4,128]{2,1,0:T(4,128)} %bitcast.5), calls=%async_computation | async-start | bytes 65536 | tf_op jit(solution)/shard_map/all_to_all | solution.py:91
  218.4 0.1 subtract_multiply_fusion
  218.5 0.1 multiply_bitcast_fusion.1
  218.6 0.1 multiply_bitcast_fusion.2
  218.8 0.1 multiply_bitcast_fusion.3
  218.8 0.2 stack.44
  219.1 0.1 fusion.14
  219.2 0.0 copy-start.4
  219.2 51.5 %reduce-scatter.9.cloned.1.call-done = f32[16,4096]{1,0:T(8,128)} async-done(((f32[256,4096]{1,0:T(8,128)}), f32[16,4096]{1,0:T(8,128)}) %reduce-scatter.9.cloned.1.call-update) | async-done | bytes 262160
  270.7 1.4 copy.90
  272.1 0.3 copy.77
  272.5 0.3 multiply_convert_fusion
  272.8 1.7 broadcast_in_dim.58
  274.5 4.8 scatter_fusion
  279.3 0.0 all-to-all-done
  279.3 0.0 copy-start.7
  279.3 7.2 %all-to-all-start.1 = ((bf16[64,9,16,128]{3,2,1,0:T(8,128)(2,1)}), bf16[64,9,16,128]{3,2,1,0:T(8,128)(2,1)S(1)}, u32[]{:S(2)}, u32[]{:S(2)}) async-start(bf16[64,9,16,128]{3,2,1,0:T(8,128)(2,1)} %scatter_fusion), calls=%async_computation.1 | async-start | bytes 4718592 | tf_op jit(solution)/shard_map/all_to_all | solution.py:90
  286.6 0.1 select_reduce_fusion
  286.7 0.7 copy.81
  287.4 0.6 compare_and_fusion
  288.0 0.6 fusion.6
  288.6 26.7 %all-to-all-done.1 = bf16[64,9,16,128]{3,2,1,0:T(8,128)(2,1)S(1)} async-done(((bf16[64,9,16,128]{3,2,1,0:T(8,128)(2,1)}), bf16[64,9,16,128]{3,2,1,0:T(8,128)(2,1)S(1)}, u32[]{:S(2)}, u32[]{:S(2)}) %all-to-all-start.1) | async-done | bytes 2359328 | tf_op jit(solution)/shard_map/all_to_all | solution.py:90
  315.3 0.4 convert_bitcast_fusion
  315.7 1.4 copy.78
  317.1 6.0 %copy.95 = f32[18,8,64,128]{3,1,2,0:T(8,128)} copy(f32[18,8,64,128]{3,2,1,0:T(8,128)S(1)} %bitcast.92) | data formatting | bytes 9437184
  323.1 7.7 %copy.79 = f32[8192,144]{1,0:T(8,128)} copy(f32[8192,144]{0,1:T(8,128)} %bitcast.91) | data formatting | bytes 9437184 | tf_op jit(solution)/shard_map/reshape | solution.py:93
  330.9 50.7 %scatter_custom_fusion.2 = f32[128,144]{1,0:T(8,128)S(1)} fusion(s32[8192]{0:T(1024)} %bitcast.102, f32[8192,144]{1,0:T(8,128)} %copy.79, f32[]{:T(128)} %constant.9.clone.1), kind=kCustom, calls=%fused_computation.25 | custom fusion | flops 1179648 | bytes 74240 | tf_op jit(solution)/shard_map/scatter-add | solution.py:94
  381.6 0.1 copy.80
  381.7 0.5 copy.82
  382.2 1.2 fusion.17
  383.4 63.4 %gather_fusion = bf16[8192,9,16]{2,1,0:T(8,128)(2,1)} fusion(bf16[9,16,128]{1,0,2:T(8,128)(2,1)S(1)} %get-tuple-element.18, s32[8192]{0:T(1024)S(1)} %copy-done.10), kind=kCustom, calls=%fused_computation | custom fusion | bytes 4751360 | tf_op jit(solution)/shard_map/jit(_take)/gather | solution.py:105
  446.7 26.8 %copy.83 = bf16[64,128,9,16]{1,3,2,0:T(8,128)(2,1)S(1)} copy(bf16[64,128,9,16]{3,2,1,0:T(8,128)(2,1)} %bitcast.90) | data formatting | bytes 4718592 | tf_op jit(solution)/shard_map/jit(_take)/gather | solution.py:105
  473.6 1.7 select_bitcast_fusion
  475.2 9.7 %all-to-all-start.2 = ((bf16[64,9,16,128]{3,2,1,0:T(8,128)(2,1)}), bf16[64,9,16,128]{3,2,1,0:T(8,128)(2,1)S(1)}, u32[]{:S(2)}, u32[]{:S(2)}) async-start(bf16[64,9,16,128]{3,2,1,0:T(8,128)(2,1)} %select_bitcast_fusion), calls=%async_computation.2 | async-start | bytes 4718592 | tf_op jit(solution)/shard_map/all_to_all | solution.py:106
  485.0 1.1 copy.85
  486.1 2.1 copy.86
  488.2 23.3 %all-to-all-done.2 = bf16[64,9,16,128]{3,2,1,0:T(8,128)(2,1)S(1)} async-done(((bf16[64,9,16,128]{3,2,1,0:T(8,128)(2,1)}), bf16[64,9,16,128]{3,2,1,0:T(8,128)(2,1)S(1)}, u32[]{:S(2)}, u32[]{:S(2)}) %all-to-all-start.2) | async-done | bytes 2359328 | tf_op jit(solution)/shard_map/all_to_all | solution.py:106
  511.5 1.7 gather_fusion.1
  513.3 1.5 convert_multiply_fusion
  514.8 0.1 slice_reduce_fusion
  514.9 0.1 slice_reduce_fusion.1
  515.0 0.8 copy-done.3
  515.7 0.9 copy_bitcast_fusion.1
  (39 shorter events, 0.1 us)
Async XLA Ops:
  7.2 61.5 %copy-start = (bf16[64,1024]{1,0:T(8,128)(2,1)S(1)}, bf16[64,1024]{1,0:T(8,128)(2,1)}, u32[]{:S(2)}) copy-start(bf16[64,1024]{1,0:T(8,128)(2,1)} %param.12) | copy-start | bytes 393220
  7.2 61.5 %all-gather.2.cloned.1.call-start = ((), (), s32[]{:S(2)}) async-start(), calls=%async_computation.5 | async-start | bytes 8912896 | tf_op jit(solution)/shard_map/all_gather | solution.py:61
  7.9 189.6 %reduce-scatter.7.cloned.1.call-start = ((), (), s32[]{:S(2)}) async-start(), calls=%async_computation.6 | async-start | bytes 17825792
  98.3 1.0 copy-start.6
  98.3 172.4 %reduce-scatter.9.cloned.1.call-start = ((), (), s32[]{:S(2)}) async-start(), calls=%async_computation.7 | async-start | bytes 4456448
  199.4 1.5 copy-start.11
  209.1 0.7 copy-start.18
  209.1 0.8 copy-start.13
  209.1 9.4 %copy-start.8 = (f32[3,4096]{1,0:T(4,128)S(1)}, f32[3,4096]{1,0:T(4,128)}, u32[]{:S(2)}) copy-start(f32[3,4096]{1,0:T(4,128)} %param.14) | copy-start | bytes 147460
  209.1 10.0 %copy-start.17 = (s32[32]{0:T(128)S(1)}, s32[32]{0:T(128)}, u32[]{:S(2)}) copy-start(s32[32]{0:T(128)} %param.17) | copy-start | bytes 388
  209.9 64.6 %copy-start.15 = (s32[32]{0:T(128)}, s32[32]{0:T(128)S(1)}, u32[]{:S(2)}) copy-start(s32[32]{0:T(128)S(1)} %fusion.15) | copy-start | bytes 388
  211.2 68.1 %all-to-all-start = ((s32[16,4,128]{2,1,0:T(4,128)}), s32[16,4,128]{2,1,0:T(4,128)S(1)}, u32[]{:S(2)}, u32[]{:S(2)}) async-start(s32[16,4,128]{2,1,0:T(4,128)} %bitcast.5), calls=%async_computation | async-start | bytes 65536 | tf_op jit(solution)/shard_map/all_to_all | solution.py:91
  219.2 55.3 %copy-start.4 = (f32[32,9,128]{2,1,0:T(8,128)}, f32[32,9,128]{2,1,0:T(8,128)S(1)}, u32[]{:S(2)}) copy-start(f32[32,9,128]{2,1,0:T(8,128)S(1)} %multiply_bitcast_fusion) | copy-start | bytes 442372
  272.5 6.8 %copy-start.2 = (f32[16,32,128]{2,0,1:T(8,128)}, f32[16,32,128]{2,0,1:T(8,128)S(1)}, u32[]{:S(2)}) copy-start(f32[16,32,128]{2,0,1:T(8,128)S(1)} %copy.77) | copy-start | bytes 786436
  279.3 7.3 %copy-start.19 = (s32[128]{0:T(128)S(1)}, s32[128]{0:T(128)}, u32[]{:S(2)}) copy-start(s32[128]{0:T(128)} %param.18) | copy-start | bytes 1540
  279.3 7.3 %copy-start.14 = (f32[4,16]{1,0:T(4,128)S(1)}, f32[4,16]{1,0:T(4,128)}, u32[]{:S(2)}) copy-start(f32[4,16]{1,0:T(4,128)} %param.19) | copy-start | bytes 772
  279.3 8.7 %copy-start.7 = (s32[16,4,128]{2,1,0:T(4,128)}, s32[16,4,128]{2,1,0:T(4,128)S(1)}, u32[]{:S(2)}) copy-start(s32[16,4,128]{2,1,0:T(4,128)S(1)} %all-to-all-done) | copy-start | bytes 98308
  279.3 36.0 %all-to-all-start.1 = ((bf16[64,9,16,128]{3,2,1,0:T(8,128)(2,1)}), bf16[64,9,16,128]{3,2,1,0:T(8,128)(2,1)S(1)}, u32[]{:S(2)}, u32[]{:S(2)}) async-start(bf16[64,9,16,128]{3,2,1,0:T(8,128)(2,1)} %scatter_fusion), calls=%async_computation.1 | async-start | bytes 4718592 | tf_op jit(solution)/shard_map/all_to_all | solution.py:90
  323.1 59.1 %copy-start.9 = (f32[16,128]{0,1:T(8,128)S(1)}, f32[16,128]{0,1:T(8,128)}, u32[]{:S(2)}) copy-start(f32[16,128]{0,1:T(8,128)} %copy.81) | copy-start | bytes 24580
  330.9 52.5 %copy-start.10 = (s32[8192]{0:T(1024)S(1)}, s32[8192]{0:T(1024)}, u32[]{:S(2)}) copy-start(s32[8192]{0:T(1024)} %fusion.6) | copy-start | bytes 98308
  446.7 26.8 %copy-start.12 = (pred[64,128]{1,0:T(8,128)(4,1)S(1)}, pred[64,128]{1,0:T(8,128)(4,1)}, u32[]{:S(2)}) copy-start(pred[64,128]{1,0:T(8,128)(4,1)} %compare_and_fusion) | copy-start | bytes 24580
  475.2 9.7 %copy-start.16 = (s32[32]{0:T(128)S(1)}, s32[32]{0:T(128)}, u32[]{:S(2)}) copy-start(s32[32]{0:T(128)} %copy-done.15) | copy-start | bytes 388
  475.2 36.3 %all-to-all-start.2 = ((bf16[64,9,16,128]{3,2,1,0:T(8,128)(2,1)}), bf16[64,9,16,128]{3,2,1,0:T(8,128)(2,1)S(1)}, u32[]{:S(2)}, u32[]{:S(2)}) async-start(bf16[64,9,16,128]{3,2,1,0:T(8,128)(2,1)} %select_bitcast_fusion), calls=%async_computation.2 | async-start | bytes 4718592 | tf_op jit(solution)/shard_map/all_to_all | solution.py:106
  486.1 27.1 %copy-start.5 = (f32[32,9,128]{2,1,0:T(8,128)S(1)}, f32[32,9,128]{2,1,0:T(8,128)}, u32[]{:S(2)}) copy-start(f32[32,9,128]{2,1,0:T(8,128)} %copy-done.4) | copy-start | bytes 442372
  513.2 3.4 copy-start.1
  514.8 1.0 copy-start.3
Sparse Core Ops, SparseCore 0:
  9.8 58.7 all-gather.1
  98.4 99.0 reduce-scatter.6
  209.2 61.4 reduce-scatter.8
where the time goes:
time: 531 us; the launch traced here: 523 us
  waiting for transfers between devices  260 us (49%)
  local copies, waits for them, and re-layouts  150 us (28%)
  other arithmetic  60.2 us (11%)
  starting transfers between devices  24.3 us (5%)
  matrix products  14.8 us (3%)
  between operations  14 us (3%)
    unnamed x5, waiting for transfers between devices  149 us
    gather x2, local copies, waits for them, and re-layouts, on_device(): looked = jnp.take(env_half, incoming_idx, axis=2).transpose(2, 0, 1, 3)  90.2 us
    all_gather x1, waiting for transfers between devices, on_device(): lax.all_gather(latent, 'tp', axis=0, tiled=True)  60.7 us
    scatter-add x1, other arithmetic, on_device(): jax.ops.segment_sum(flattened, incoming_idx.reshape(-1), num_segments=ato...  50.7 us
    unnamed x48, local copies, waits for them, and re-layouts  39.3 us
    all_to_all x1, waiting for transfers between devices, on_device(): lax.all_to_all(outgoing, 'dom', split_axis=0, concat_axis=0, tiled=True)  26.7 us
    all_to_all x1, waiting for transfers between devices, on_device(): lax.all_to_all(looked, 'dom', split_axis=0, concat_axis=0, tiled=True)  23.3 us
    dot_general x2, matrix products, contract_rows(): lax.dot_general(left, right, (((0,), (0,)), ((), ())), preferred_element_...  14.8 us
  transfers between devices with their start and end apart: 6, of which 5 were waited for; matrix products, arithmetic and copies ran while one was open for 3% of the time, Pallas kernels for 0%

commit v1 on v0

v1 whole, which is shorter than its diff:
```python
import math

import jax
import jax.numpy as jnp
from jax import lax
from jax.experimental import pallas as pl
from jax.experimental.pallas import tpu as pltpu
from jax.sharding import PartitionSpec as P

MESH = pl.DeviceIdType.MESH
F32 = jnp.float32
BF16 = jnp.bfloat16

root_three = math.sqrt(3.0)
root_five = math.sqrt(5.0)
root_fifteen = math.sqrt(15.0)
cutoff_radius = 6.0
env_factor = 0.25

SIDE = 4
NDOM = 16
NTP = 16


def dot(left, right, dims):
    return lax.dot_general(left, right, (dims, ((), ())), preferred_element_type=F32)


def kernel(
    dest_ref, fill_ref, latent, w1, w2, we, ev_ref, cen_ref, spec_ref, gain_ref,
    ln_out, env_out, inv_out,
    w1_part, pieces, ring, g1, g2, ge, x_in, x_t, hid, lnt, ln, ws, wt, hs, onehot, slots,
    sums, p_out, p_in, table,
    pre_sem, lat_send, lat_recv, one_send, one_recv, a_send, a_recv, b_send, b_recv,
    sib_send, sib_recv, w_send, w_recv, ln_send, ln_recv, q_send, q_recv, t_send, t_recv,
):
    dom = lax.axis_index("dom")
    me = lax.axis_index("tp")
    ax = dom // SIDE
    by = dom % SIDE
    core = me % 2
    sib = me + 1 - 2 * core

    def tp_peer(k):
        return (me + k) % NTP

    def dom_peer(k):
        return (dom + k) % NDOM

    def remote(src, dst, send, recv, to_dom, to_tp):
        return pltpu.make_async_remote_copy(
            src_ref=src, dst_ref=dst, send_sem=send, recv_sem=recv,
            device_id=(to_dom, to_tp), device_id_type=MESH,
        )

    pre = [
        pltpu.make_async_copy(w1.at[pl.ds(by * 256, 256), :], w1_part, pre_sem.at[0]),
        pltpu.make_async_copy(
            latent.at[:, pl.ds(pl.multiple_of(me * 256, 256), 256)], x_in.at[me], pre_sem.at[1]
        ),
    ]
    for half in range(2):
        lanes = pl.ds(pl.multiple_of(by * 256 + 128 * half, 128), 128)
        pre.append(
            pltpu.make_async_copy(
                w2.at[pl.ds(ax * 16, 16), lanes], pieces.at[half, 1], pre_sem.at[2 + half]
            )
        )
        pre.append(
            pltpu.make_async_copy(
                we.at[pl.ds(by * 16, 16), pl.ds(128 * half, 128)],
                pieces.at[half, 2], pre_sem.at[4 + half],
            )
        )
    for copy in pre:
        copy.start()

    barrier = pltpu.get_barrier_semaphore()

    def greet(k, carry):
        pl.semaphore_signal(barrier, inc=1, device_id=(dom, tp_peer(k)), device_id_type=MESH)
        pl.semaphore_signal(barrier, inc=1, device_id=(dom_peer(k), me), device_id_type=MESH)
        return carry

    lax.fori_loop(1, NTP, greet, 0)
    for copy in pre:
        copy.wait()
    pick = (
        lax.broadcasted_iota(jnp.int32, (16, 64), 1)
        == lax.broadcasted_iota(jnp.int32, (16, 64), 0) + ax * 16
    ).astype(F32).astype(BF16)
    turned = dot(pick, w1_part[...], ((1,), (1,))).astype(BF16)
    pieces[0, 0] = turned[:, :128]
    pieces[1, 0] = turned[:, 128:]
    pl.semaphore_wait(barrier, NTP - 1 + NDOM - 1)

    ring[pl.ds(me, 1)] = pieces[pl.ds(core, 1)]

    def one_copy(k):
        to = tp_peer(k)
        return remote(pieces.at[to % 2], ring.at[me], one_send.at[k], one_recv.at[k], dom, to)

    def lat_copy(k):
        to = tp_peer(k)
        return remote(
            latent.at[:, pl.ds(pl.multiple_of(to * 256, 256), 256)], x_in.at[me],
            lat_send.at[k], lat_recv.at[k], dom, to,
        )

    def w_copy(k):
        to = tp_peer(k)
        return remote(ws.at[to], wt.at[me], w_send.at[k], w_recv.at[k], dom, to)

    def ln_copy(k):
        to = tp_peer(k)
        return remote(
            ln.at[to], ln_out.at[:, pl.ds(pl.multiple_of(me * 256, 256), 256)],
            ln_send.at[k], ln_recv.at[k], dom, to,
        )

    def q_copy(k):
        to = dom_peer(k)
        return remote(p_out.at[to], p_in.at[dom], q_send.at[k], q_recv.at[k], to, me)

    def t_copy(k):
        to = dom_peer(k)
        return remote(table.at[dom], table.at[dom], t_send.at[k], t_recv.at[k], to, me)

    def start_all(make):
        def body(k, carry):
            make(k).start()
            return carry

        lax.fori_loop(1, 16, body, 0)

    def recv_all(make):
        def body(k, carry):
            make(k).wait_recv()
            return carry

        lax.fori_loop(1, 16, body, 0)

    def send_all(make):
        def body(k, carry):
            make(k).wait_send()
            return carry

        lax.fori_loop(1, 16, body, 0)

    start_all(one_copy)
    start_all(lat_copy)
    recv_all(one_copy)

    def x_peer(k):
        return ((ax + k) % SIDE) * SIDE + by

    def y_peer(k):
        return ax * SIDE + (by + k) % SIDE

    g1[pl.ds(core, 1), pl.ds(by, 1), pl.ds(ax, 1)] = ring[:, 0][None, None, None]
    g2[pl.ds(core, 1), pl.ds(ax, 1), pl.ds(by, 1)] = ring[:, 1][None, None, None]
    ge[pl.ds(core, 1), :, pl.ds(by, 1)] = ring[:, 2][None, :, None]
    first = []
    for k in range(1, SIDE):
        one = g1.at[core, by, ax]
        first.append(remote(one, one, a_send.at[0, k], a_recv.at[0, k], x_peer(k), me))
        two = g2.at[core, ax, by]
        first.append(remote(two, two, a_send.at[1, k], a_recv.at[1, k], y_peer(k), me))
        three = ge.at[core, :, by]
        first.append(
            remote(ring.at[:, 2], three, a_send.at[2, k], a_recv.at[2, k], y_peer(k), me)
        )
    for copy in first:
        copy.start()

    def harmonics(t, carry):
        v = ev_ref[:, pl.ds(pl.multiple_of(t * 256, 256), 256)]
        along_x, along_y, along_z = v[0:1], v[1:2], v[2:3]
        radius = jnp.sqrt(along_x * along_x + along_y * along_y + along_z * along_z)
        ux = along_x / radius
        uy = along_y / radius
        uz = along_z / radius
        ratio = radius / cutoff_radius
        flat = 1.0 - ratio * ratio
        envelope = flat * flat
        spot = lax.broadcasted_iota(jnp.int32, (1, 128), 1)
        alive = jnp.concatenate(
            [(spot < fill_ref[2 * t + j]).astype(F32) for j in range(2)], axis=1
        )
        rows = [
            envelope,
            root_three * ux * envelope,
            root_three * uy * envelope,
            root_three * uz * envelope,
            root_fifteen * ux * uy * envelope,
            root_fifteen * uy * uz * envelope,
            root_five / 2.0 * (3.0 * uz * uz - 1.0) * envelope,
            root_fifteen * ux * uz * envelope,
            root_fifteen / 2.0 * (ux * ux - uy * uy) * envelope,
            alive,
        ]
        for m, row in enumerate(rows):
            hs[t, m : m + 1, :] = row
        return carry

    lax.fori_loop(0, NTP, harmonics, 0)

    for k in range(SIDE - 1):
        first[3 * k].wait_recv()
        first[3 * k + 1].wait_recv()
    second = []
    for k in range(1, SIDE):
        one = g1.at[core, by]
        second.append(remote(one, one, b_send.at[0, k], b_recv.at[0, k], y_peer(k), me))
        two = g2.at[core, ax]
        second.append(remote(two, two, b_send.at[1, k], b_recv.at[1, k], x_peer(k), me))
    for copy in second:
        copy.start()

    def sib_copy(ref, kind, k):
        return remote(ref, ref, sib_send.at[kind, k], sib_recv.at[kind, k], dom, sib)

    across = [sib_copy(g1.at[core, by], 0, 0), sib_copy(g2.at[core, ax], 1, 0)]
    for copy in across:
        copy.start()

    def make_onehot(b, carry):
        atoms = lax.broadcasted_iota(jnp.int32, (128, 128), 0)
        onehot[b] = (atoms == cen_ref[pl.ds(b, 1), :]).astype(F32).astype(BF16)
        return carry

    lax.fori_loop(0, 32, make_onehot, 0)

    def make_slots(d, carry):
        found = [jnp.int32(32)] * 4
        for b in range(32):
            hit = dest_ref[b, 0] == d
            found = [jnp.where(hit, new, old) for new, old in zip([b] + found[:3], found)]
        for s in range(4):
            slots[4 * d + s] = found[s]
        return carry

    lax.fori_loop(0, NDOM, make_slots, 0)
    sums[32] = jnp.zeros((144, 128), F32)
    same = lax.broadcasted_iota(jnp.int32, (16, 16), 0) == lax.broadcasted_iota(
        jnp.int32, (16, 16), 1
    )
    gain = jnp.zeros((16, 128), F32)
    for s in range(4):
        column = jnp.sum(jnp.where(same, gain_ref[s : s + 1, :], 0.0), axis=1, keepdims=True)
        gain = gain + jnp.where(spec_ref[...] == s, column, 0.0)

    for k in range(SIDE - 1):
        first[3 * k + 2].wait_recv()
    last = sib_copy(ge.at[core], 2, 0)
    last.start()
    across.append(last)

    for k in range(1, SIDE):
        second[2 * k - 2].wait_recv()
        copy = sib_copy(g1.at[core, (by - k + SIDE) % SIDE], 0, k)
        copy.start()
        across.append(copy)
        second[2 * k - 1].wait_recv()
        copy = sib_copy(g2.at[core, (ax - k + SIDE) % SIDE], 1, k)
        copy.start()
        across.append(copy)

    recv_all(lat_copy)
    for n in range(4):
        block = x_in[4 * n : 4 * n + 4].reshape(256, 256).astype(F32)
        x_t[:, 256 * n : 256 * n + 256] = block.T.astype(BF16)

    other = 1 - core

    def sib_arrival(ref, kind, k):
        remote(ref, ref, sib_send.at[kind, k], sib_recv.at[kind, k], dom, sib).wait_recv()

    sib_arrival(g1.at[other, by], 0, 0)
    for k in range(1, SIDE):
        sib_arrival(g1.at[other, (by - k + SIDE) % SIDE], 0, k)

    def first_layer(r, carry):
        matrix = jnp.concatenate(
            [g1[c, b, r].reshape(256, 128) for b in range(SIDE) for c in range(2)], axis=1
        )
        v = dot(x_t[...], matrix, ((1,), (1,)))
        hid[r] = (v / (1.0 + jnp.exp(-v))).astype(BF16)
        return carry

    lax.fori_loop(0, SIDE, first_layer, 0)

    sib_arrival(g2.at[other, ax], 1, 0)
    for k in range(1, SIDE):
        sib_arrival(g2.at[other, (ax - k + SIDE) % SIDE], 1, k)

    for b in range(SIDE):
        update = jnp.zeros((256, 256), F32)
        for r in range(SIDE):
            matrix = jnp.concatenate([g2[c, r, b].reshape(256, 128) for c in range(2)], axis=1)
            update = update + dot(hid[r], matrix, ((1,), (0,)))
        lanes = slice(256 * b, 256 * b + 256)
        lnt[:, lanes] = (x_t[:, lanes].astype(F32) + update).astype(BF16)

    sib_arrival(ge.at[other], 2, 0)
    matrix = jnp.concatenate([ge[c].reshape(1024, 128) for c in range(2)], axis=1)
    env_weights = dot(lnt[...], matrix, ((1,), (0,)))
    ws[...] = env_weights.T.astype(BF16).reshape(16, 16, 256)
    wt[pl.ds(me, 1)] = ws[pl.ds(me, 1)]
    start_all(w_copy)

    for b in range(SIDE):
        block = lnt[:, 256 * b : 256 * b + 256].astype(F32).T.astype(BF16)
        ln[4 * b : 4 * b + 4] = block.reshape(4, 64, 256)
    own = pltpu.make_async_copy(
        ln.at[me], ln_out.at[:, pl.ds(pl.multiple_of(me * 256, 256), 256)], pre_sem.at[6]
    )
    own.start()
    start_all(ln_copy)

    recv_all(w_copy)

    def block_sums(t, carry):
        w = wt[t].astype(F32)
        h = hs[t]
        for j in range(2):
            lanes = slice(128 * j, 128 * j + 128)
            wj = w[:, lanes]
            alive = h[9:10, lanes]
            contrib = jnp.concatenate(
                [((h[m : m + 1, lanes] * wj) * alive).astype(BF16) for m in range(9)], axis=0
            )
            sums[2 * t + j] = dot(contrib, onehot[2 * t + j], ((1,), (1,)))
        return carry

    lax.fori_loop(0, NTP, block_sums, 0)

    def domain_sum(d):
        total = sums[slots[4 * d]] + sums[slots[4 * d + 1]]
        return total + (sums[slots[4 * d + 2]] + sums[slots[4 * d + 3]])

    def send_sums(k, carry):
        to = dom_peer(k)
        p_out[to] = domain_sum(to).astype(BF16)
        q_copy(k).start()
        return carry

    lax.fori_loop(1, NDOM, send_sums, 0)
    total = domain_sum(dom)
    recv_all(q_copy)

    def add(k, total):
        return total + p_in[(dom + k) % NDOM].astype(F32)

    total = lax.fori_loop(1, NDOM, add, total)
    env = total.reshape(9, 16, 128) * gain[None] * env_factor
    env_out[...] = env
    table[pl.ds(dom, 1)] = env.reshape(1, 144, 128).astype(BF16)
    start_all(t_copy)
    recv_all(t_copy)

    def finish(t, carry):
        w = wt[t].astype(F32)
        h = hs[t]
        parts = [[], [], []]
        for j in range(2):
            lanes = slice(128 * j, 128 * j + 128)
            env_edge = dot(table[dest_ref[2 * t + j, 0]], onehot[2 * t + j], ((1,), (0,)))
            terms = [
                env_edge[16 * m : 16 * m + 16] * h[m : m + 1, lanes] for m in range(9)
            ]
            degrees = [
                terms[0],
                terms[1] + terms[2] + terms[3],
                terms[4] + terms[5] + terms[6] + terms[7] + terms[8],
            ]
            for l in range(3):
                parts[l].append(degrees[l] * w[:, lanes] * h[9:10, lanes])
        for l in range(3):
            inv_out[l, :, pl.ds(pl.multiple_of(t * 256, 256), 256)] = jnp.concatenate(
                parts[l], axis=1
            )
        return carry

    lax.fori_loop(0, NTP, finish, 0)

    own.wait()
    recv_all(ln_copy)
    for copy in first + second + across:
        copy.wait_send()
    for make in (one_copy, lat_copy, w_copy, ln_copy, q_copy, t_copy):
        send_all(make)


def on_device(
    latent, w_first, w_second, w_env, edge_vec, centers, block_dest, block_fill, species,
    species_gain,
):
    smem = pl.BlockSpec(memory_space=pltpu.SMEM)
    vmem = pl.BlockSpec(memory_space=pltpu.VMEM)
    anywhere = pl.BlockSpec(memory_space=pl.ANY)
    dma = pltpu.SemaphoreType.DMA
    return pl.pallas_call(
        kernel,
        out_shape=(
            jax.ShapeDtypeStruct((64, 4096), BF16),
            jax.ShapeDtypeStruct((9, 16, 128), F32),
            jax.ShapeDtypeStruct((3, 16, 4096), F32),
        ),
        in_specs=[smem, smem, anywhere, anywhere, anywhere, anywhere, vmem, vmem, vmem, vmem],
        out_specs=(anywhere, vmem, vmem),
        scratch_shapes=[
            pltpu.VMEM((256, 64), BF16),
            pltpu.VMEM((2, 3, 16, 128), BF16),
            pltpu.VMEM((16, 3, 16, 128), BF16),
            pltpu.VMEM((2, 4, 4, 16, 16, 128), BF16),
            pltpu.VMEM((2, 4, 4, 16, 16, 128), BF16),
            pltpu.VMEM((2, 16, 4, 16, 128), BF16),
            pltpu.VMEM((16, 64, 256), BF16),
            pltpu.VMEM((256, 1024), BF16),
            pltpu.VMEM((4, 256, 256), BF16),
            pltpu.VMEM((256, 1024), BF16),
            pltpu.VMEM((16, 64, 256), BF16),
            pltpu.VMEM((16, 16, 256), BF16),
            pltpu.VMEM((16, 16, 256), BF16),
            pltpu.VMEM((16, 16, 256), F32),
            pltpu.VMEM((32, 128, 128), BF16),
            pltpu.SMEM((64,), jnp.int32),
            pltpu.VMEM((33, 144, 128), F32),
            pltpu.VMEM((16, 144, 128), BF16),
            pltpu.VMEM((16, 144, 128), BF16),
            pltpu.VMEM((16, 144, 128), BF16),
            dma((8,)),
            dma((16,)), dma((16,)), dma((16,)), dma((16,)),
            dma((3, 4)), dma((3, 4)), dma((2, 4)), dma((2, 4)), dma((3, 4)), dma((3, 4)),
            dma((16,)), dma((16,)), dma((16,)), dma((16,)),
            dma((16,)), dma((16,)), dma((16,)), dma((16,)),
        ],
        compiler_params=pltpu.CompilerParams(
            collective_id=0, has_side_effects=True, vmem_limit_bytes=40 * 1024 * 1024
        ),
        cost_estimate=pl.CostEstimate(
            flops=2 * 10**9, bytes_accessed=4 * 10**6, transcendentals=300000
        ),
        name="allegro",
    )(
        block_dest, block_fill, latent, w_first, w_second, w_env, edge_vec,
        centers.reshape(32, 128), species.reshape(1, 128), species_gain,
    )


def solution(mesh):
    in_specs = (
        P("tp", "dom"),
        P(None, "tp"),
        P("tp", None),
        P("tp", None),
        P(None, "dom"),
        P("dom"),
        P("dom", None),
        P("dom"),
        P("dom"),
        P(None, "tp"),
    )
    out_specs = (P("tp", "dom"), P(None, "tp", "dom"), P(None, "tp", "dom"))
    return jax.shard_map(
        on_device, mesh=mesh, in_specs=in_specs, out_specs=out_specs, check_vma=False
    )
```

time: 531 us -> 87.2 us (0.16); the launches traced: 523 us -> 87 us
  waiting for transfers between devices: 260 us -> 0 us
  local copies, waits for them, and re-layouts: 150 us -> 5.3 us
  Pallas kernels: 0 us -> 81 us
  other arithmetic: 60.2 us -> 0 us
  starting transfers between devices: 24.3 us -> 0 us
  matrix products: 14.8 us -> 0 us
  between operations: 14 us -> 0.75 us
    unnamed x5 -> x0, waiting for transfers between devices: 149 us -> none
    gather x3 -> x0, local copies, waits for them, and re-layouts: 91.9 us -> none  [the longest x2 90.2 us: on_device(): looked = jnp.take(env_half, incoming_idx, axis=2).transpose(2, 0, 1, 3)]
    pallas_call x0 -> x1, Pallas kernels: none -> 81 us  [on_device(): pl.pallas_call(kernel, out_shape=(jax.ShapeDtypeStruct((64, 4096), BF16),...]
    all_gather x1 -> x0, waiting for transfers between devices: 60.7 us -> none  [on_device(): lax.all_gather(latent, 'tp', axis=0, tiled=True)]
    scatter-add x1 -> x0, other arithmetic: 50.7 us -> none  [on_device(): jax.ops.segment_sum(flattened, incoming_idx.reshape(-1), num_segments=ato...]
    all_to_all x3 -> x0, waiting for transfers between devices: 50 us -> none  [the longest x1 26.7 us: on_device(): lax.all_to_all(outgoing, 'dom', split_axis=0, concat_axis=0, tiled=True)]
    unnamed x48 -> x23, local copies, waits for them, and re-layouts: 39.3 us -> 5.3 us
    all_to_all x3 -> x0, starting transfers between devices: 24.2 us -> none  [the longest x1 9.72 us: on_device(): lax.all_to_all(looked, 'dom', split_axis=0, concat_axis=0, tiled=True)]
  transfers between devices with their start and end apart: 6 -> 0, of which waited for: 5 -> 0; matrix products, arithmetic and copies ran while one was open for 3% -> 0% of each run, Pallas kernels for 0% -> 0%
where the time goes in v1:
time: 87.2 us; the launch traced here: 87 us
  Pallas kernels  81 us (93%)
  local copies, waits for them, and re-layouts  5.3 us (6%)
    pallas_call x1, Pallas kernels, on_device(): pl.pallas_call(kernel, out_shape=(jax.ShapeDtypeStruct((64, 4096), BF16),...  81 us
    unnamed x23, local copies, waits for them, and re-layouts  5.3 us

profile of v1, /device:TPU:8, one launch (start us, length us, event | category | flops | bytes accessed | tf_op | source)
XLA Modules:
  0.0 87.0 jit_solution(387949134548844127)
XLA Ops:
  0.6 0.0 copy-start.8
  0.6 0.6 copy-done.8
  1.3 0.1 copy.13.dest_ref
  1.4 0.0 copy-start.1
  1.4 0.0 copy-start.2
  1.4 0.0 copy-start.3
  1.4 0.0 copy-start.4
  1.4 0.0 copy-start.5
  1.4 0.0 copy-start.6
  1.4 0.0 copy-start.7
  1.4 1.2 %copy.14.w1 = bf16[1024,64]{1,0:T(8,128)(2,1)S(1)} copy(bf16[1024,64]{0,1:T(8,128)(2,1)} %param.11) | data formatting | bytes 262144 | tf_op args[1]
  2.6 0.0 copy-done.1
  2.6 0.0 copy-done.2
  2.6 0.0 copy-done.3
  2.7 0.0 copy-done.4
  2.7 0.0 copy-done.5
  2.7 0.0 copy-done.6
  2.7 0.0 copy-done.7
  2.7 0.0 copy-start
  2.7 1.0 %copy-done = bf16[64,4096]{1,0:T(8,128)(2,1)S(1)} copy-done((bf16[64,4096]{1,0:T(8,128)(2,1)S(1)}, bf16[64,4096]{1,0:T(8,128)(2,1)}, u32[]{:S(2)}) %copy-start) | copy-done | bytes 524312
  3.7 81.0 %allegro.1 = (bf16[64,4096]{1,0:T(8,128)(2,1)S(1)}, f32[9,16,128]{2,1,0:T(8,128)S(1)}, f32[3,16,4096]{2,1,0:T(8,128)S(1)}) custom-call(s32[32,1]{1,0:T(8,128)S(1)} %copy.13.dest_ref, s32[32]{0:T(128)S(1)} %copy-done.6, bf16[64,4096]{1,0:T(8,128)(2,1)S(1)} %copy-done, bf16[1024,64]{1,0:T(8,128)(2,1)S(1)} %copy.14.w1, bf16[64,1024]{1,0:T(8,128)(2,1)S(1)} %copy-done.1, ...), custom_call_target="tpu_custom_call" | custom-call | flops 2000000000 | bytes 4000000 | tf_op jit(solution)/shard_map/allegro/pallas_call | solution.py:403
  84.7 0.8 copy.18
  85.5 0.6 copy.19
  86.1 0.9 %copy.20 = f32[3,16,4096]{2,1,0:T(8,128)} copy(f32[3,16,4096]{2,1,0:T(8,128)S(1)} %get-tuple-element.8) | data formatting | bytes 1572864
Async XLA Ops:
  0.6 0.7 copy-start.8
  1.4 1.3 %copy-start.1 = (bf16[64,1024]{1,0:T(8,128)(2,1)S(1)}, bf16[64,1024]{1,0:T(8,128)(2,1)}, u32[]{:S(2)}) copy-start(bf16[64,1024]{1,0:T(8,128)(2,1)} %w2.1) | copy-start | bytes 393220
  1.4 1.3 %copy-start.2 = (f32[3,4096]{1,0:T(4,128)S(1)}, f32[3,4096]{1,0:T(4,128)}, u32[]{:S(2)}) copy-start(f32[3,4096]{1,0:T(4,128)} %ev_ref.1) | copy-start | bytes 147460
  1.4 1.3 %copy-start.3 = (bf16[64,256]{1,0:T(8,128)(2,1)S(1)}, bf16[64,256]{1,0:T(8,128)(2,1)}, u32[]{:S(2)}) copy-start(bf16[64,256]{1,0:T(8,128)(2,1)} %we.1) | copy-start | bytes 98308
  1.4 1.3 %copy-start.4 = (s32[4096]{0:T(1024)S(1)}, s32[4096]{0:T(1024)}, u32[]{:S(2)}) copy-start(s32[4096]{0:T(1024)} %param.15) | copy-start | bytes 49156
  1.4 1.3 %copy-start.5 = (f32[4,16]{1,0:T(4,128)S(1)}, f32[4,16]{1,0:T(4,128)}, u32[]{:S(2)}) copy-start(f32[4,16]{1,0:T(4,128)} %gain_ref.1) | copy-start | bytes 772
  1.4 1.3 %copy-start.6 = (s32[32]{0:T(128)S(1)}, s32[32]{0:T(128)}, u32[]{:S(2)}) copy-start(s32[32]{0:T(128)} %fill_ref.1) | copy-start | bytes 388
  1.4 1.3 %copy-start.7 = (s32[128]{0:T(128)S(1)}, s32[128]{0:T(128)}, u32[]{:S(2)}) copy-start(s32[128]{0:T(128)} %param.18) | copy-start | bytes 1540
  2.7 1.0 %copy-start = (bf16[64,4096]{1,0:T(8,128)(2,1)S(1)}, bf16[64,4096]{1,0:T(8,128)(2,1)}, u32[]{:S(2)}) copy-start(bf16[64,4096]{1,0:T(8,128)(2,1)} %latent.1) | copy-start | bytes 1572868

commit v2 on v1

v2 whole, which is shorter than its diff:
```python
import math

import jax
import jax.numpy as jnp
from jax import lax
from jax.experimental import pallas as pl
from jax.experimental.pallas import tpu as pltpu
from jax.sharding import PartitionSpec as P

MESH = pl.DeviceIdType.MESH
F32 = jnp.float32
BF16 = jnp.bfloat16

root_three = math.sqrt(3.0)
root_five = math.sqrt(5.0)
root_fifteen = math.sqrt(15.0)
cutoff_radius = 6.0
env_factor = 0.25

SIDE = 4
NDOM = 16
NTP = 16
DEPTH = 8
HALF = DEPTH // 2
NEAR_Z = (7, 6, 2, 1, 5, 4, 3)
FAR = sorted(
    [(dx, dy) for dx in range(SIDE) for dy in range(SIDE) if dx or dy],
    key=lambda d: -min(d[0], SIDE - d[0]) - min(d[1], SIDE - d[1]),
)


def dot(left, right, dims):
    return lax.dot_general(left, right, (dims, ((), ())), preferred_element_type=F32)


def kernel(
    dest_ref, fill_ref, latent, w1, w2, we, ev_ref, cen_ref, spec_ref, gain_ref,
    ln_out, env_out, inv_out,
    pieces, ring, own1, own2, g1, g2, ge, x_in, x_t, hid, lnt, ln, ws, wt, hs, onehot, slots,
    sums, p_low, p_high, in_low, in_high, table_low, table_high,
    pre_sem, lat_send, lat_recv, one_send, one_recv, own_send, own_recv,
    a_send, a_recv, b_send, b_recv, e_send, e_recv,
    sib_send, sib_recv, w_send, w_recv, ln_send, ln_recv, q_send, q_recv, t_send, t_recv,
):
    dom = lax.axis_index("dom")
    me = lax.axis_index("tp")
    ax = dom // SIDE
    by = dom % SIDE
    core = me % 2
    other = 1 - core
    z = me // 2
    sib = 2 * z + other

    def tp_far(q):
        s = q // 2
        dz = HALF + (s + 1) // 2 * (1 - 2 * (s % 2))
        return 2 * ((z + dz) % DEPTH) + (core + 1 + q) % 2

    def tp_source(q):
        s = q // 2
        dz = HALF + (s + 1) // 2 * (1 - 2 * (s % 2))
        return 2 * ((z + DEPTH - dz) % DEPTH) + (core + 1 + q) % 2

    def dom_far(q):
        dx, dy = FAR[q]
        return (ax + dx) % SIDE * SIDE + (by + dy) % SIDE

    def x_peer(k):
        return (ax + k) % SIDE * SIDE + by

    def y_peer(k):
        return ax * SIDE + (by + k) % SIDE

    def remote(src, dst, send, recv, to_dom, to_tp):
        return pltpu.make_async_remote_copy(
            src_ref=src, dst_ref=dst, send_sem=send, recv_sem=recv,
            device_id=(to_dom, to_tp), device_id_type=MESH,
        )

    def each(count, act):
        def body(q, carry):
            act(q)
            return carry

        lax.fori_loop(0, count, body, 0)

    pre = [
        pltpu.make_async_copy(
            latent.at[:, pl.ds(pl.multiple_of(me * 256, 256), 256)], x_in.at[me], pre_sem.at[7]
        ),
        pltpu.make_async_copy(w1, own1.at[core], pre_sem.at[8]),
        pltpu.make_async_copy(w2, own2.at[core], pre_sem.at[9]),
    ]
    for half in range(2):
        lanes = pl.ds(pl.multiple_of(by * 256 + 128 * half, 128), 128)
        for i, matrix in enumerate([w1, w2]):
            pre.append(
                pltpu.make_async_copy(
                    matrix.at[pl.ds(ax * 16, 16), lanes],
                    pieces.at[half, i], pre_sem.at[2 * i + half],
                )
            )
        pre.append(
            pltpu.make_async_copy(
                we.at[pl.ds(by * 16, 16), pl.ds(128 * half, 128)],
                pieces.at[half, 2], pre_sem.at[4 + half],
            )
        )
    for copy in pre:
        copy.start()

    barrier = pltpu.get_barrier_semaphore()

    def greet_tp(q):
        pl.semaphore_signal(barrier, inc=1, device_id=(dom, tp_far(q)), device_id_type=MESH)

    each(NTP - 1, greet_tp)
    for q in range(NDOM - 1):
        pl.semaphore_signal(barrier, inc=1, device_id=(dom_far(q), me), device_id_type=MESH)
    for copy in pre:
        copy.wait()
    ring[pl.ds(14 + core, 1)] = pieces[pl.ds(core, 1)]
    pl.semaphore_wait(barrier, NTP - 1 + NDOM - 1)

    def one_copy(n, c):
        to = 2 * ((z + NEAR_Z[n]) % DEPTH) + c
        return remote(
            pieces.at[c], ring.at[2 * n + core], one_send.at[2 * n + c],
            one_recv.at[2 * n + core], dom, to,
        )

    def one_arrival(slot):
        remote(
            pieces.at[0], ring.at[slot], one_send.at[slot], one_recv.at[slot], dom, sib
        ).wait_recv()

    tile_copies = [one_copy(n, c) for n in range(7) for c in range(2)]
    tile_copies.append(
        remote(
            pieces.at[other], ring.at[14 + core], one_send.at[14], one_recv.at[14], dom, sib
        )
    )
    own_copies = [
        remote(ref.at[core], ref.at[core], own_send.at[i], own_recv.at[i], dom, sib)
        for i, ref in enumerate([own1, own2])
    ]
    for copy in tile_copies + own_copies:
        copy.start()

    def lat_copy(q):
        to = tp_far(q)
        return remote(
            latent.at[:, pl.ds(pl.multiple_of(to * 256, 256), 256)], x_in.at[me],
            lat_send.at[q], lat_recv.at[q], dom, to,
        )

    def w_copy(q):
        to = tp_far(q)
        return remote(ws.at[to], wt.at[me], w_send.at[q], w_recv.at[q], dom, to)

    def ln_copy(q):
        to = tp_far(q)
        return remote(
            ln.at[to], ln_out.at[:, pl.ds(pl.multiple_of(me * 256, 256), 256)],
            ln_send.at[q], ln_recv.at[q], dom, to,
        )

    each(15, lambda q: lat_copy(q).start())

    groups = [slice(0, 8), slice(8, 14)]
    spans = [pl.ds(0, 8), pl.ds(8, 6)]
    first = []
    for g in range(2):
        for slot in range(groups[g].start, groups[g].stop):
            one_arrival(slot)
        tiles = ring[groups[g]]
        g1[pl.ds(core, 1), pl.ds(by, 1), pl.ds(ax, 1), groups[g]] = tiles[:, 0][None, None, None]
        g2[pl.ds(core, 1), pl.ds(ax, 1), pl.ds(by, 1), groups[g]] = tiles[:, 1][None, None, None]
        copies = []
        for k in (2, 1, 3):
            one = g1.at[core, by, ax, spans[g]]
            copies.append(remote(one, one, a_send.at[g, 0, k], a_recv.at[g, 0, k], x_peer(k), me))
            two = g2.at[core, ax, by, spans[g]]
            copies.append(remote(two, two, a_send.at[g, 1, k], a_recv.at[g, 1, k], y_peer(k), me))
        for copy in copies:
            copy.start()
        first.append(copies)
    tile_copies[14].wait_recv()
    for n in range(7):
        for c in range(2):
            chip = (z + DEPTH - NEAR_Z[n]) % DEPTH
            ge[pl.ds(core, 1), pl.ds(2 * chip + c, 1), pl.ds(by, 1)] = ring[2 * n + c, 2][
                None, None, None
            ]
    for c in range(2):
        ge[pl.ds(core, 1), pl.ds(2 * z + c, 1), pl.ds(by, 1)] = ring[14 + c, 2][None, None, None]
    env_copies = []
    for k in (2, 1, 3):
        three = ge.at[core, :, by]
        env_copies.append(remote(three, three, e_send.at[k], e_recv.at[k], y_peer(k), me))
    for copy in env_copies:
        copy.start()

    def sib_copy(g, kind, k):
        ref = (
            g1.at[core, (by + SIDE - k) % SIDE, :, spans[g]]
            if kind == 0
            else g2.at[core, (ax + SIDE - k) % SIDE, :, spans[g]]
        )
        return remote(
            ref, ref, sib_send.at[g, kind, k], sib_recv.at[g, kind, k], dom, sib
        )

    second = []
    across = []
    for g in range(2):
        for copy in first[g]:
            copy.wait_recv()
        copies = []
        for k in (2, 1, 3):
            one = g1.at[core, by, :, spans[g]]
            copies.append(remote(one, one, b_send.at[g, 0, k], b_recv.at[g, 0, k], y_peer(k), me))
            two = g2.at[core, ax, :, spans[g]]
            copies.append(remote(two, two, b_send.at[g, 1, k], b_recv.at[g, 1, k], x_peer(k), me))
        for copy in copies:
            copy.start()
        second.append(copies)
        for kind in range(2):
            copy = sib_copy(g, kind, 0)
            copy.start()
            across.append(copy)

    def harmonics(t):
        v = ev_ref[:, pl.ds(pl.multiple_of(t * 256, 256), 256)]
        along_x, along_y, along_z = v[0:1], v[1:2], v[2:3]
        radius = jnp.sqrt(along_x * along_x + along_y * along_y + along_z * along_z)
        ux = along_x / radius
        uy = along_y / radius
        uz = along_z / radius
        ratio = radius / cutoff_radius
        flat = 1.0 - ratio * ratio
        envelope = flat * flat
        spot = lax.broadcasted_iota(jnp.int32, (1, 128), 1)
        alive = jnp.concatenate(
            [(spot < fill_ref[2 * t + j]).astype(F32) for j in range(2)], axis=1
        )
        rows = [
            envelope,
            root_three * ux * envelope,
            root_three * uy * envelope,
            root_three * uz * envelope,
            root_fifteen * ux * uy * envelope,
            root_fifteen * uy * uz * envelope,
            root_five / 2.0 * (3.0 * uz * uz - 1.0) * envelope,
            root_fifteen * ux * uz * envelope,
            root_fifteen / 2.0 * (ux * ux - uy * uy) * envelope,
            alive,
        ]
        for m, row in enumerate(rows):
            hs[t, m : m + 1, :] = row

    each(NTP, harmonics)

    def make_onehot(b):
        atoms = lax.broadcasted_iota(jnp.int32, (128, 128), 0)
        onehot[b] = (atoms == cen_ref[pl.ds(b, 1), :]).astype(F32).astype(BF16)

    each(32, make_onehot)

    def make_slots(d):
        found = [jnp.int32(32)] * 4
        for b in range(32):
            hit = dest_ref[b] == d
            found = [jnp.where(hit, new, old) for new, old in zip([b] + found[:3], found)]
        for s in range(4):
            slots[4 * d + s] = found[s]

    each(NDOM, make_slots)
    sums[32] = jnp.zeros((144, 128), F32)
    same = lax.broadcasted_iota(jnp.int32, (16, 16), 0) == lax.broadcasted_iota(
        jnp.int32, (16, 16), 1
    )
    gain = jnp.zeros((16, 128), F32)
    for s in range(4):
        column = jnp.sum(jnp.where(same, gain_ref[s : s + 1, :], 0.0), axis=1, keepdims=True)
        gain = gain + jnp.where(spec_ref[...] == s, column, 0.0)

    for copy in env_copies:
        copy.wait_recv()
    last = remote(ge.at[core], ge.at[core], own_send.at[2], own_recv.at[2], dom, sib)
    last.start()
    across.append(last)
    for g in range(2):
        for i, k in enumerate((2, 1, 3)):
            for kind in range(2):
                second[g][2 * i + kind].wait_recv()
                copy = sib_copy(g, kind, k)
                copy.start()
                across.append(copy)
        if g == 0:
            each(15, lambda q: lat_copy(q).wait_recv())
            for n in range(4):
                block = x_in[4 * n : 4 * n + 4].reshape(256, 256).astype(F32)
                x_t[:, 256 * n : 256 * n + 256] = block.T.astype(BF16)

    def sib_arrivals(kind):
        own_copies[kind].wait_recv()
        for g in range(2):
            for k in range(SIDE):
                sib_copy(g, kind, k).wait_recv()

    sib_arrivals(0)

    def first_layer(r):
        tiles = jnp.concatenate(
            [g1[c, b, r].reshape(224, 128) for b in range(SIDE) for c in range(2)], axis=1
        )
        rows = pl.ds(pl.multiple_of(16 * r, 16), 16)
        matrix = jnp.concatenate([tiles, own1[0, rows, :], own1[1, rows, :]], axis=0)
        v = dot(x_t[...], matrix, ((1,), (1,)))
        hid[r] = (v / (1.0 + jnp.exp(-v))).astype(BF16)

    each(SIDE, first_layer)
    sib_arrivals(1)
    for b in range(SIDE):
        lanes = slice(256 * b, 256 * b + 256)
        update = jnp.zeros((256, 256), F32)
        for r in range(SIDE):
            tiles = jnp.concatenate([g2[c, r, b].reshape(224, 128) for c in range(2)], axis=1)
            rows = slice(16 * r, 16 * r + 16)
            matrix = jnp.concatenate([tiles, own2[0, rows, lanes], own2[1, rows, lanes]], axis=0)
            update = update + dot(hid[r], matrix, ((1,), (0,)))
        lnt[:, lanes] = (x_t[:, lanes].astype(F32) + update).astype(BF16)

    last.wait_recv()
    matrix = jnp.concatenate([ge[c].reshape(1024, 128) for c in range(2)], axis=1)
    env_weights = dot(lnt[...], matrix, ((1,), (0,)))
    ws[...] = env_weights.T.astype(BF16).reshape(16, 16, 256)
    each(15, lambda q: w_copy(q).start())
    wt[pl.ds(me, 1)] = ws[pl.ds(me, 1)]

    for b in range(SIDE):
        block = lnt[:, 256 * b : 256 * b + 256].astype(F32).T.astype(BF16)
        ln[4 * b : 4 * b + 4] = block.reshape(4, 64, 256)
    own = pltpu.make_async_copy(
        ln.at[me], ln_out.at[:, pl.ds(pl.multiple_of(me * 256, 256), 256)], pre_sem.at[6]
    )
    own.start()
    each(15, lambda q: ln_copy(q).start())

    def block_sums(t):
        w = wt[t].astype(F32)
        h = hs[t]
        for j in range(2):
            lanes = slice(128 * j, 128 * j + 128)
            wj = w[:, lanes]
            alive = h[9:10, lanes]
            contrib = jnp.concatenate(
                [((h[m : m + 1, lanes] * wj) * alive).astype(BF16) for m in range(9)], axis=0
            )
            sums[2 * t + j] = dot(contrib, onehot[2 * t + j], ((1,), (1,)))

    block_sums(me)

    def arrived_sums(q):
        w_copy(14 - q).wait_recv()
        block_sums(tp_source(14 - q))

    each(15, arrived_sums)

    def domain_sum(d):
        total = sums[slots[4 * d]] + sums[slots[4 * d + 1]]
        return total + (sums[slots[4 * d + 2]] + sums[slots[4 * d + 3]])

    def q_copy(part, q):
        out, into = ((p_low, in_low), (p_high, in_high))[part]
        to = dom_far(q)
        return remote(
            out.at[to], into.at[dom], q_send.at[part, q], q_recv.at[part, q], to, me
        )

    def t_copy(part, q):
        ref = (table_low, table_high)[part]
        return remote(
            ref.at[dom], ref.at[dom], t_send.at[part, q], t_recv.at[part, q], dom_far(q), me
        )

    for q in range(NDOM - 1):
        to = dom_far(q)
        total = domain_sum(to).astype(BF16)
        p_low[pl.ds(to, 1)] = total[None, :64]
        p_high[pl.ds(to, 1)] = total[None, 64:]
        q_copy(0, q).start()
    for q in range(NDOM - 1):
        q_copy(1, q).start()
    total = domain_sum(dom)
    for part in range(2):
        into, ref = ((in_low, table_low), (in_high, table_high))[part]
        rows = (slice(0, 64), slice(64, 144))[part]
        comps = (slice(0, 4), slice(4, 9))[part]
        for q in range(NDOM - 1):
            q_copy(part, q).wait_recv()

        def add(k, acc):
            return acc + into[(dom + k) % NDOM].astype(F32)

        acc = lax.fori_loop(1, NDOM, add, total[rows])
        env = acc.reshape(-1, 16, 128) * gain[None] * env_factor
        ref[pl.ds(dom, 1)] = env.reshape(1, -1, 128).astype(BF16)
        for q in range(NDOM - 1):
            t_copy(part, q).start()
        env_out[comps] = env

    def finish(t, part):
        w = wt[t].astype(F32)
        h = hs[t]
        ref = (table_low, table_high)[part]
        base = (0, 4)[part]
        spans_of = (((0,), (1, 2, 3)), ((4, 5, 6, 7, 8),))[part]
        parts = [[] for _ in spans_of]
        for j in range(2):
            lanes = slice(128 * j, 128 * j + 128)
            env_edge = dot(ref[dest_ref[2 * t + j]], onehot[2 * t + j], ((1,), (0,)))
            for l, comps in enumerate(spans_of):
                degree = None
                for m in comps:
                    term = env_edge[16 * (m - base) : 16 * (m - base) + 16] * h[m : m + 1, lanes]
                    degree = term if degree is None else degree + term
                parts[l].append(degree * w[:, lanes] * h[9:10, lanes])
        for l in range(len(spans_of)):
            inv_out[(0, 2)[part] + l, :, pl.ds(pl.multiple_of(t * 256, 256), 256)] = (
                jnp.concatenate(parts[l], axis=1)
            )

    for part in range(2):
        for q in range(NDOM - 1):
            t_copy(part, q).wait_recv()
        each(NTP, lambda t: finish(t, part))

    own.wait()
    each(15, lambda q: ln_copy(q).wait_recv())
    for copy in tile_copies + own_copies + first[0] + first[1] + env_copies:
        copy.wait_send()
    for copy in second[0] + second[1] + across:
        copy.wait_send()
    for make in (lat_copy, w_copy, ln_copy):
        each(15, lambda q: make(q).wait_send())
    for part in range(2):
        for q in range(NDOM - 1):
            q_copy(part, q).wait_send()
            t_copy(part, q).wait_send()


def on_device(
    latent, w_first, w_second, w_env, edge_vec, centers, block_dest, block_fill, species,
    species_gain,
):
    smem = pl.BlockSpec(memory_space=pltpu.SMEM)
    vmem = pl.BlockSpec(memory_space=pltpu.VMEM)
    hbm = pl.BlockSpec(memory_space=pltpu.HBM)
    dma = pltpu.SemaphoreType.DMA
    return pl.pallas_call(
        kernel,
        out_shape=(
            jax.ShapeDtypeStruct((64, 4096), BF16),
            jax.ShapeDtypeStruct((9, 16, 128), F32),
            jax.ShapeDtypeStruct((3, 16, 4096), F32),
        ),
        in_specs=[smem, smem, hbm, hbm, hbm, hbm, vmem, vmem, vmem, vmem],
        out_specs=(vmem, vmem, vmem),
        scratch_shapes=[
            pltpu.VMEM((2, 3, 16, 128), BF16),
            pltpu.VMEM((16, 3, 16, 128), BF16),
            pltpu.VMEM((2, 64, 1024), BF16),
            pltpu.VMEM((2, 64, 1024), BF16),
            pltpu.VMEM((2, 4, 4, 14, 16, 128), BF16),
            pltpu.VMEM((2, 4, 4, 14, 16, 128), BF16),
            pltpu.VMEM((2, 16, 4, 16, 128), BF16),
            pltpu.VMEM((16, 64, 256), BF16),
            pltpu.VMEM((256, 1024), BF16),
            pltpu.VMEM((4, 256, 256), BF16),
            pltpu.VMEM((256, 1024), BF16),
            pltpu.VMEM((16, 64, 256), BF16),
            pltpu.VMEM((16, 16, 256), BF16),
            pltpu.VMEM((16, 16, 256), BF16),
            pltpu.VMEM((16, 16, 256), F32),
            pltpu.VMEM((32, 128, 128), BF16),
            pltpu.SMEM((64,), jnp.int32),
            pltpu.VMEM((33, 144, 128), F32),
            pltpu.VMEM((16, 64, 128), BF16),
            pltpu.VMEM((16, 80, 128), BF16),
            pltpu.VMEM((16, 64, 128), BF16),
            pltpu.VMEM((16, 80, 128), BF16),
            pltpu.VMEM((16, 64, 128), BF16),
            pltpu.VMEM((16, 80, 128), BF16),
            dma((10,)),
            dma((15,)), dma((15,)), dma((15,)), dma((15,)), dma((3,)), dma((3,)),
            dma((2, 2, 4)), dma((2, 2, 4)), dma((2, 2, 4)), dma((2, 2, 4)), dma((4,)), dma((4,)),
            dma((2, 2, 4)), dma((2, 2, 4)),
            dma((15,)), dma((15,)), dma((15,)), dma((15,)),
            dma((2, 15)), dma((2, 15)), dma((2, 15)), dma((2, 15)),
        ],
        compiler_params=pltpu.CompilerParams(
            collective_id=0, has_side_effects=True, vmem_limit_bytes=60 * 1024 * 1024
        ),
        cost_estimate=pl.CostEstimate(
            flops=2 * 10**9, bytes_accessed=4 * 10**6, transcendentals=300000
        ),
        name="allegro",
    )(
        block_dest.reshape(32), block_fill, latent, w_first.T, w_second, w_env, edge_vec,
        centers.reshape(32, 128), species.reshape(1, 128), species_gain,
    )


def solution(mesh):
    in_specs = (
        P("tp", "dom"),
        P(None, "tp"),
        P("tp", None),
        P("tp", None),
        P(None, "dom"),
        P("dom"),
        P("dom", None),
        P("dom"),
        P("dom"),
        P(None, "tp"),
    )
    out_specs = (P("tp", "dom"), P(None, "tp", "dom"), P(None, "tp", "dom"))
    return jax.shard_map(
        on_device, mesh=mesh, in_specs=in_specs, out_specs=out_specs, check_vma=False
    )
```

time: 87.2 us -> 79.4 us (0.911); the launches traced: 87 us -> 78.2 us
  Pallas kernels: 81 us -> 74.1 us
  local copies, waits for them, and re-layouts: 5.3 us -> 3.48 us
    pallas_call x1, Pallas kernels: 81 us -> 74.1 us  [on_device(): pl.pallas_call(kernel, out_shape=(jax.ShapeDtypeStruct((64, 4096), BF16),...]
    unnamed x23 -> x7, local copies, waits for them, and re-layouts: 5.3 us -> 3.48 us
where the time goes in v2:
time: 79.4 us; the launch traced here: 78.2 us
  Pallas kernels  74.1 us (93%)
  local copies, waits for them, and re-layouts  3.48 us (4%)
    pallas_call x1, Pallas kernels, on_device(): pl.pallas_call(kernel, out_shape=(jax.ShapeDtypeStruct((64, 4096), BF16),...  74.1 us
    unnamed x7, local copies, waits for them, and re-layouts  3.48 us

profile of v2, /device:TPU:8, one launch (start us, length us, event | category | flops | bytes accessed | tf_op | source)
XLA Modules:
  0.0 78.2 jit_solution(8037574407477663158)
XLA Ops:
  0.6 74.1 %allegro.1 = (bf16[64,4096]{1,0:T(8,128)(2,1)}, f32[9,16,128]{2,1,0:T(8,128)}, f32[3,16,4096]{2,1,0:T(8,128)}) custom-call(s32[32]{0:T(128)} %bitcast.6, s32[32]{0:T(128)} %fill_ref.1, bf16[64,4096]{1,0:T(8,128)(2,1)} %latent.1, bf16[64,1024]{1,0:T(8,128)(2,1)} %bitcast.4, bf16[64,1024]{1,0:T(8,128)(2,1)} %w2.1, bf16[64,256]{1,0:T(8,128)(2,1)} %we.1, ...), custom_call_target="tpu_custom_call" | custom-call | flops 2000000000 | bytes 4000000 | tf_op jit(solution)/shard_map/allegro/pallas_call | solution.py:462
  74.7 0.0 copy-start
  74.7 0.0 copy-start.1
  74.7 2.0 %copy.16 = bf16[64,4096]{1,0:T(8,128)(2,1)} copy(bf16[64,4096]{1,0:T(8,128)(2,1)} %get-tuple-element.6) | data formatting | bytes 1048576
  76.7 0.0 copy-done.1
  76.7 0.6 copy.17
  77.3 0.0 copy-done
  77.3 0.9 %copy.18 = f32[3,16,4096]{2,1,0:T(8,128)} copy(f32[3,16,4096]{2,1,0:T(8,128)S(1)} %copy-done) | data formatting | bytes 1572864
Async XLA Ops:
  74.7 2.6 %copy-start = (f32[3,16,4096]{2,1,0:T(8,128)S(1)}, f32[3,16,4096]{2,1,0:T(8,128)}, u32[]{:S(2)}) copy-start(f32[3,16,4096]{2,1,0:T(8,128)} %get-tuple-element.8) | copy-start | bytes 2359300
  74.7 2.0 %copy-start.1 = (f32[9,16,128]{2,1,0:T(8,128)S(1)}, f32[9,16,128]{2,1,0:T(8,128)}, u32[]{:S(2)}) copy-start(f32[9,16,128]{2,1,0:T(8,128)} %get-tuple-element.7) | copy-start | bytes 221188

commit v3 on v2

--- a/solution.py
+++ b/solution.py
@@ -22,7 +22,7 @@
 NTP = 16
 DEPTH = 8
 HALF = DEPTH // 2
-NEAR_Z = (7, 6, 2, 1, 5, 4, 3)
+NEAR_Z = (6, 2, 7, 1, 4, 5, 3)
 FAR = sorted(
     [(dx, dy) for dx in range(SIDE) for dy in range(SIDE) if dx or dy],
     key=lambda d: -min(d[0], SIDE - d[0]) - min(d[1], SIDE - d[1]),
@@ -34,8 +34,9 @@
 
 
 def kernel(
-    dest_ref, fill_ref, latent, w1, w2, we, ev_ref, cen_ref, spec_ref, gain_ref,
+    dest, fill, latent, w1, w2, we, ev, cen, spec, gains,
     ln_out, env_out, inv_out,
+    dest_ref, fill_ref, ev_ref, cen_ref, spec_ref, gain_ref,
     pieces, ring, own1, own2, g1, g2, ge, x_in, x_t, hid, lnt, ln, ws, wt, hs, onehot, slots,
     sums, p_low, p_high, in_low, in_high, table_low, table_high,
     pre_sem, lat_send, lat_recv, one_send, one_recv, own_send, own_recv,
@@ -77,12 +78,12 @@
             device_id=(to_dom, to_tp), device_id_type=MESH,
         )
 
-    def each(count, act):
+    def each(count, act, unroll=1):
         def body(q, carry):
             act(q)
             return carry
 
-        lax.fori_loop(0, count, body, 0)
+        lax.fori_loop(0, count, body, 0, unroll=unroll)
 
     pre = [
         pltpu.make_async_copy(
@@ -109,6 +110,17 @@
     for copy in pre:
         copy.start()
 
+    small = [
+        pltpu.make_async_copy(src, dst, pre_sem.at[10 + i])
+        for i, (src, dst) in enumerate(
+            [
+                (dest, dest_ref), (fill, fill_ref), (ev, ev_ref), (cen, cen_ref),
+                (spec, spec_ref), (gains, gain_ref),
+            ]
+        )
+    ]
+    for copy in small:
+        copy.start()
     barrier = pltpu.get_barrier_semaphore()
 
     def greet_tp(q):
@@ -165,11 +177,22 @@
             ln_send.at[q], ln_recv.at[q], dom, to,
         )
 
-    each(15, lambda q: lat_copy(q).start())
-
     groups = [slice(0, 8), slice(8, 14)]
     spans = [pl.ds(0, 8), pl.ds(8, 6)]
+
+    def sib_copy(g, kind, k):
+        ref = (
+            g1.at[core, (by + SIDE - k) % SIDE, :, spans[g]]
+            if kind == 0
+            else g2.at[core, (ax + SIDE - k) % SIDE, :, spans[g]]
+        )
+        return remote(
+            ref, ref, sib_send.at[g, kind, k], sib_recv.at[g, kind, k], dom, sib
+        )
+
     first = []
+    second = []
+    across = []
     for g in range(2):
         for slot in range(groups[g].start, groups[g].stop):
             one_arrival(slot)
@@ -185,6 +208,24 @@
         for copy in copies:
             copy.start()
         first.append(copies)
+        if g == 1:
+            each(15, lambda q: lat_copy(q).start())
+        for copy in copies:
+            copy.wait_recv()
+        copies = []
+        for k in (2, 1, 3):
+            one = g1.at[core, by, :, spans[g]]
+            copies.append(remote(one, one, b_send.at[g, 0, k], b_recv.at[g, 0, k], y_peer(k), me))
+            two = g2.at[core, ax, :, spans[g]]
+            copies.append(remote(two, two, b_send.at[g, 1, k], b_recv.at[g, 1, k], x_peer(k), me))
+        for copy in copies:
+            copy.start()
+        second.append(copies)
+        for kind in range(2):
+            copy = sib_copy(g, kind, 0)
+            copy.start()
+            across.append(copy)
+
     tile_copies[14].wait_recv()
     for n in range(7):
         for c in range(2):
@@ -201,34 +242,8 @@
     for copy in env_copies:
         copy.start()
 
-    def sib_copy(g, kind, k):
-        ref = (
-            g1.at[core, (by + SIDE - k) % SIDE, :, spans[g]]
-            if kind == 0
-            else g2.at[core, (ax + SIDE - k) % SIDE, :, spans[g]]
-        )
-        return remote(
-            ref, ref, sib_send.at[g, kind, k], sib_recv.at[g, kind, k], dom, sib
-        )
-
-    second = []
-    across = []
-    for g in range(2):
-        for copy in first[g]:
-            copy.wait_recv()
-        copies = []
-        for k in (2, 1, 3):
-            one = g1.at[core, by, :, spans[g]]
-            copies.append(remote(one, one, b_send.at[g, 0, k], b_recv.at[g, 0, k], y_peer(k), me))
-            two = g2.at[core, ax, :, spans[g]]
-            copies.append(remote(two, two, b_send.at[g, 1, k], b_recv.at[g, 1, k], x_peer(k), me))
-        for copy in copies:
-            copy.start()
-        second.append(copies)
-        for kind in range(2):
-            copy = sib_copy(g, kind, 0)
-            copy.start()
-            across.append(copy)
+    for copy in small:
+        copy.wait()
 
     def harmonics(t):
         v = ev_ref[:, pl.ds(pl.multiple_of(t * 256, 256), 256)]
@@ -342,12 +357,6 @@
     for b in range(SIDE):
         block = lnt[:, 256 * b : 256 * b + 256].astype(F32).T.astype(BF16)
         ln[4 * b : 4 * b + 4] = block.reshape(4, 64, 256)
-    own = pltpu.make_async_copy(
-        ln.at[me], ln_out.at[:, pl.ds(pl.multiple_of(me * 256, 256), 256)], pre_sem.at[6]
-    )
-    own.start()
-    each(15, lambda q: ln_copy(q).start())
-
     def block_sums(t):
         w = wt[t].astype(F32)
         h = hs[t]
@@ -393,6 +402,11 @@
         q_copy(0, q).start()
     for q in range(NDOM - 1):
         q_copy(1, q).start()
+    own = pltpu.make_async_copy(
+        ln.at[me], ln_out.at[:, pl.ds(pl.multiple_of(me * 256, 256), 256)], pre_sem.at[6]
+    )
+    own.start()
+    each(15, lambda q: ln_copy(q).start())
     total = domain_sum(dom)
     for part in range(2):
         into, ref = ((in_low, table_low), (in_high, table_high))[part]
@@ -435,7 +449,7 @@
     for part in range(2):
         for q in range(NDOM - 1):
             t_copy(part, q).wait_recv()
-        each(NTP, lambda t: finish(t, part))
+        each(NTP, lambda t: finish(t, part), unroll=4)
 
     own.wait()
     each(15, lambda q: ln_copy(q).wait_recv())
@@ -451,24 +465,52 @@
             t_copy(part, q).wait_send()
 
 
+def write_out(ln_in, env_in, inv_in, ln_out, env_out, inv_out, ln, env, inv, sem_in, sem_out):
+    parts = [(env_in, env, env_out)]
+    for n in range(2):
+        rows = pl.ds(32 * n, 32)
+        parts.append((ln_in.at[rows], ln.at[rows], ln_out.at[rows]))
+    for l in range(3):
+        parts.append((inv_in.at[l], inv.at[l], inv_out.at[l]))
+    reads = [
+        pltpu.make_async_copy(src, mid, sem_in.at[n]) for n, (src, mid, _) in enumerate(parts)
+    ]
+    writes = [
+        pltpu.make_async_copy(mid, dst, sem_out.at[n]) for n, (_, mid, dst) in enumerate(parts)
+    ]
+    for copy in reads:
+        copy.start()
+    for read, write in zip(reads, writes):
+        read.wait()
+        write.start()
+    for copy in writes:
+        copy.wait()
+
+
 def on_device(
     latent, w_first, w_second, w_env, edge_vec, centers, block_dest, block_fill, species,
     species_gain,
 ):
-    smem = pl.BlockSpec(memory_space=pltpu.SMEM)
     vmem = pl.BlockSpec(memory_space=pltpu.VMEM)
     hbm = pl.BlockSpec(memory_space=pltpu.HBM)
     dma = pltpu.SemaphoreType.DMA
-    return pl.pallas_call(
+    shapes = (
+        jax.ShapeDtypeStruct((64, 4096), BF16),
+        jax.ShapeDtypeStruct((9, 16, 128), F32),
+        jax.ShapeDtypeStruct((3, 16, 4096), F32),
+    )
+    results = pl.pallas_call(
         kernel,
-        out_shape=(
-            jax.ShapeDtypeStruct((64, 4096), BF16),
-            jax.ShapeDtypeStruct((9, 16, 128), F32),
-            jax.ShapeDtypeStruct((3, 16, 4096), F32),
-        ),
-        in_specs=[smem, smem, hbm, hbm, hbm, hbm, vmem, vmem, vmem, vmem],
+        out_shape=shapes,
+        in_specs=[hbm] * 10,
         out_specs=(vmem, vmem, vmem),
         scratch_shapes=[
+            pltpu.SMEM((32,), jnp.int32),
+            pltpu.SMEM((32,), jnp.int32),
+            pltpu.VMEM((3, 4096), F32),
+            pltpu.VMEM((32, 128), jnp.int32),
+            pltpu.VMEM((1, 128), jnp.int32),
+            pltpu.VMEM((4, 16), F32),
             pltpu.VMEM((2, 3, 16, 128), BF16),
             pltpu.VMEM((16, 3, 16, 128), BF16),
             pltpu.VMEM((2, 64, 1024), BF16),
@@ -493,7 +535,7 @@
             pltpu.VMEM((16, 80, 128), BF16),
             pltpu.VMEM((16, 64, 128), BF16),
             pltpu.VMEM((16, 80, 128), BF16),
-            dma((10,)),
+            dma((16,)),
             dma((15,)), dma((15,)), dma((15,)), dma((15,)), dma((3,)), dma((3,)),
             dma((2, 2, 4)), dma((2, 2, 4)), dma((2, 2, 4)), dma((2, 2, 4)), dma((4,)), dma((4,)),
             dma((2, 2, 4)), dma((2, 2, 4)),
@@ -511,6 +553,21 @@
         block_dest.reshape(32), block_fill, latent, w_first.T, w_second, w_env, edge_vec,
         centers.reshape(32, 128), species.reshape(1, 128), species_gain,
     )
+    return pl.pallas_call(
+        write_out,
+        out_shape=shapes,
+        in_specs=[hbm] * 3,
+        out_specs=(hbm,) * 3,
+        scratch_shapes=[
+            pltpu.VMEM((64, 4096), BF16),
+            pltpu.VMEM((9, 16, 128), F32),
+            pltpu.VMEM((3, 16, 4096), F32),
+            dma((6,)),
+            dma((6,)),
+        ],
+        compiler_params=pltpu.CompilerParams(vmem_limit_bytes=60 * 1024 * 1024),
+        name="write_out",
+    )(*results)
 
 
 def solution(mesh):

time: 79.4 us -> 75 us (0.945)
  local copies, waits for them, and re-layouts: 3.48 us -> 0 us
    unnamed x7 -> x0, local copies, waits for them, and re-layouts: 3.48 us -> none
    pallas_call x1 -> x2, Pallas kernels: 74.1 us -> 73.6 us  [the longest x1 71.4 us: on_device(): pl.pallas_call(kernel, out_shape=shapes, in_specs=[hbm] * 10, out_specs=(...]
where the time goes in v3:
time: 75 us; the launch traced here: 74.2 us
  Pallas kernels  73.6 us (98%)
    pallas_call x1, Pallas kernels, on_device(): pl.pallas_call(kernel, out_shape=shapes, in_specs=[hbm] * 10, out_specs=(...  71.4 us
    pallas_call x1, Pallas kernels, on_device(): pl.pallas_call(write_out, out_shape=shapes, in_specs=[hbm] * 3, out_specs...  2.14 us

profile of v3, /device:TPU:8, one launch (start us, length us, event | category | flops | bytes accessed | tf_op | source)
XLA Modules:
  0.0 74.2 jit_solution(11428409106558507478)
XLA Ops:
  0.6 71.4 %allegro.1 = (bf16[64,4096]{1,0:T(8,128)(2,1)}, f32[9,16,128]{2,1,0:T(8,128)}, f32[3,16,4096]{2,1,0:T(8,128)}) custom-call(s32[32]{0:T(128)} %bitcast.6, s32[32]{0:T(128)} %fill.1, bf16[64,4096]{1,0:T(8,128)(2,1)} %latent.1, bf16[64,1024]{1,0:T(8,128)(2,1)} %bitcast.4, bf16[64,1024]{1,0:T(8,128)(2,1)} %w2.1, bf16[64,256]{1,0:T(8,128)(2,1)} %we.1, ...), custom_call_target="tpu_custom_call" | custom-call | flops 2000000000 | bytes 4000000 | tf_op jit(solution)/shard_map/allegro/pallas_call | solution.py:502
  72.0 2.1 %write_out.1 = (bf16[64,4096]{1,0:T(8,128)(2,1)}, f32[9,16,128]{2,1,0:T(8,128)}, f32[3,16,4096]{2,1,0:T(8,128)}) custom-call(bf16[64,4096]{1,0:T(8,128)(2,1)} %get-tuple-element.6.ln_in, f32[9,16,128]{2,1,0:T(8,128)} %get-tuple-element.7.env_in, f32[3,16,4096]{2,1,0:T(8,128)} %get-tuple-element.8.inv_in), custom_call_target="tpu_custom_call" | custom-call | tf_op jit(solution)/shard_map/write_out/pallas_call | solution.py:556

commit v4 on v3

--- a/solution.py
+++ b/solution.py
@@ -57,11 +57,6 @@
         dz = HALF + (s + 1) // 2 * (1 - 2 * (s % 2))
         return 2 * ((z + dz) % DEPTH) + (core + 1 + q) % 2
 
-    def tp_source(q):
-        s = q // 2
-        dz = HALF + (s + 1) // 2 * (1 - 2 * (s % 2))
-        return 2 * ((z + DEPTH - dz) % DEPTH) + (core + 1 + q) % 2
-
     def dom_far(q):
         dx, dy = FAR[q]
         return (ax + dx) % SIDE * SIDE + (by + dy) % SIDE
@@ -103,7 +98,7 @@
             )
         pre.append(
             pltpu.make_async_copy(
-                we.at[pl.ds(by * 16, 16), pl.ds(128 * half, 128)],
+                we.at[pl.ds((by, ax)[half] * 16, 16), pl.ds(128 * half, 128)],
                 pieces.at[half, 2], pre_sem.at[4 + half],
             )
         )
@@ -177,22 +172,70 @@
             ln_send.at[q], ln_recv.at[q], dom, to,
         )
 
+    for copy in small:
+        copy.wait()
+
+    def harmonics(t):
+        v = ev_ref[:, pl.ds(pl.multiple_of(t * 256, 256), 256)]
+        along_x, along_y, along_z = v[0:1], v[1:2], v[2:3]
+        radius = jnp.sqrt(along_x * along_x + along_y * along_y + along_z * along_z)
+        ux = along_x / radius
+        uy = along_y / radius
+        uz = along_z / radius
+        ratio = radius / cutoff_radius
+        flat = 1.0 - ratio * ratio
+        envelope = flat * flat
+        spot = lax.broadcasted_iota(jnp.int32, (1, 128), 1)
+        alive = jnp.concatenate(
+            [(spot < fill_ref[2 * t + j]).astype(F32) for j in range(2)], axis=1
+        )
+        rows = [
+            envelope,
+            root_three * ux * envelope,
+            root_three * uy * envelope,
+            root_three * uz * envelope,
+            root_fifteen * ux * uy * envelope,
+            root_fifteen * uy * uz * envelope,
+            root_five / 2.0 * (3.0 * uz * uz - 1.0) * envelope,
+            root_fifteen * ux * uz * envelope,
+            root_fifteen / 2.0 * (ux * ux - uy * uy) * envelope,
+            alive,
+        ]
+        for m, row in enumerate(rows):
+            hs[t, m : m + 1, :] = row
+
+    each(NTP, harmonics)
+
+    def make_onehot(b):
+        atoms = lax.broadcasted_iota(jnp.int32, (128, 128), 0)
+        onehot[b] = (atoms == cen_ref[pl.ds(b, 1), :]).astype(F32).astype(BF16)
+
+    each(32, make_onehot)
+
     groups = [slice(0, 8), slice(8, 14)]
     spans = [pl.ds(0, 8), pl.ds(8, 6)]
 
-    def sib_copy(g, kind, k):
-        ref = (
-            g1.at[core, (by + SIDE - k) % SIDE, :, spans[g]]
-            if kind == 0
-            else g2.at[core, (ax + SIDE - k) % SIDE, :, spans[g]]
-        )
+    def quad(g, kind, k, half=None):
+        part = slice(None) if half is None else pl.ds(2 * half, 2)
+        if kind == 0:
+            return g1.at[core, (by + SIDE - k) % SIDE, part, spans[g]]
+        return g2.at[core, (ax + SIDE - k) % SIDE, part, spans[g]]
+
+    def sib_copy(g, kind, k, half=None):
+        ref = quad(g, kind, k, half)
+        slot = k if half is None else 2 + 2 * half
         return remote(
-            ref, ref, sib_send.at[g, kind, k], sib_recv.at[g, kind, k], dom, sib
-        )
+            ref, ref, sib_send.at[g, kind, slot], sib_recv.at[g, kind, slot], dom, sib
+        )
+
+    def second_peer(kind, k):
+        return (y_peer, x_peer)[kind](k)
 
     first = []
     second = []
     across = []
+    env_row = by * other + ax * core
+    env_copies = []
     for g in range(2):
         for slot in range(groups[g].start, groups[g].stop):
             one_arrival(slot)
@@ -210,77 +253,39 @@
         first.append(copies)
         if g == 1:
             each(15, lambda q: lat_copy(q).start())
+            tile_copies[14].wait_recv()
+            for n in range(7):
+                for c in range(2):
+                    chip = (z + DEPTH - NEAR_Z[n]) % DEPTH
+                    ge[pl.ds(core, 1), pl.ds(2 * chip + c, 1), pl.ds(env_row, 1)] = ring[
+                        2 * n + c, 2
+                    ][None, None, None]
+            for c in range(2):
+                ge[pl.ds(core, 1), pl.ds(2 * z + c, 1), pl.ds(env_row, 1)] = ring[14 + c, 2][
+                    None, None, None
+                ]
+            for k in (2, 1, 3):
+                three = ge.at[core, :, env_row]
+                to = (ax + k * core) % SIDE * SIDE + (by + k * other) % SIDE
+                env_copies.append(remote(three, three, e_send.at[k], e_recv.at[k], to, me))
+            for copy in env_copies:
+                copy.start()
         for copy in copies:
             copy.wait_recv()
-        copies = []
-        for k in (2, 1, 3):
-            one = g1.at[core, by, :, spans[g]]
-            copies.append(remote(one, one, b_send.at[g, 0, k], b_recv.at[g, 0, k], y_peer(k), me))
-            two = g2.at[core, ax, :, spans[g]]
-            copies.append(remote(two, two, b_send.at[g, 1, k], b_recv.at[g, 1, k], x_peer(k), me))
-        for copy in copies:
-            copy.start()
+        copies = {}
+        for k in (1, 3):
+            for kind in range(2):
+                mine = quad(g, kind, 0)
+                copies[kind, k] = remote(
+                    mine, mine, b_send.at[g, kind, k], b_recv.at[g, kind, k],
+                    second_peer(kind, k), me,
+                )
+                copies[kind, k].start()
         second.append(copies)
         for kind in range(2):
             copy = sib_copy(g, kind, 0)
             copy.start()
             across.append(copy)
-
-    tile_copies[14].wait_recv()
-    for n in range(7):
-        for c in range(2):
-            chip = (z + DEPTH - NEAR_Z[n]) % DEPTH
-            ge[pl.ds(core, 1), pl.ds(2 * chip + c, 1), pl.ds(by, 1)] = ring[2 * n + c, 2][
-                None, None, None
-            ]
-    for c in range(2):
-        ge[pl.ds(core, 1), pl.ds(2 * z + c, 1), pl.ds(by, 1)] = ring[14 + c, 2][None, None, None]
-    env_copies = []
-    for k in (2, 1, 3):
-        three = ge.at[core, :, by]
-        env_copies.append(remote(three, three, e_send.at[k], e_recv.at[k], y_peer(k), me))
-    for copy in env_copies:
-        copy.start()
-
-    for copy in small:
-        copy.wait()
-
-    def harmonics(t):
-        v = ev_ref[:, pl.ds(pl.multiple_of(t * 256, 256), 256)]
-        along_x, along_y, along_z = v[0:1], v[1:2], v[2:3]
-        radius = jnp.sqrt(along_x * along_x + along_y * along_y + along_z * along_z)
-        ux = along_x / radius
-        uy = along_y / radius
-        uz = along_z / radius
-        ratio = radius / cutoff_radius
-        flat = 1.0 - ratio * ratio
-        envelope = flat * flat
-        spot = lax.broadcasted_iota(jnp.int32, (1, 128), 1)
-        alive = jnp.concatenate(
-            [(spot < fill_ref[2 * t + j]).astype(F32) for j in range(2)], axis=1
-        )
-        rows = [
-            envelope,
-            root_three * ux * envelope,
-            root_three * uy * envelope,
-            root_three * uz * envelope,
-            root_fifteen * ux * uy * envelope,
-            root_fifteen * uy * uz * envelope,
-            root_five / 2.0 * (3.0 * uz * uz - 1.0) * envelope,
-            root_fifteen * ux * uz * envelope,
-            root_fifteen / 2.0 * (ux * ux - uy * uy) * envelope,
-            alive,
-        ]
-        for m, row in enumerate(rows):
-            hs[t, m : m + 1, :] = row
-
-    each(NTP, harmonics)
-
-    def make_onehot(b):
-        atoms = lax.broadcasted_iota(jnp.int32, (128, 128), 0)
-        onehot[b] = (atoms == cen_ref[pl.ds(b, 1), :]).astype(F32).astype(BF16)
-
-    each(32, make_onehot)
 
     def make_slots(d):
         found = [jnp.int32(32)] * 4
@@ -290,39 +295,58 @@
         for s in range(4):
             slots[4 * d + s] = found[s]
 
-    each(NDOM, make_slots)
-    sums[32] = jnp.zeros((144, 128), F32)
-    same = lax.broadcasted_iota(jnp.int32, (16, 16), 0) == lax.broadcasted_iota(
-        jnp.int32, (16, 16), 1
-    )
-    gain = jnp.zeros((16, 128), F32)
-    for s in range(4):
-        column = jnp.sum(jnp.where(same, gain_ref[s : s + 1, :], 0.0), axis=1, keepdims=True)
-        gain = gain + jnp.where(spec_ref[...] == s, column, 0.0)
-
+    relays = []
+    for g in range(2):
+        copies = {}
+        for half, k in enumerate((1, 3)):
+            for kind in range(2):
+                second[g][kind, k].wait_recv()
+                theirs = quad(g, kind, k, half)
+                copies[kind, half] = remote(
+                    theirs, theirs, b_send.at[g, kind, 2 * half], b_recv.at[g, kind, 2 * half],
+                    second_peer(kind, k), me,
+                )
+                copies[kind, half].start()
+        relays.append(copies)
+        for k in (1, 3):
+            for kind in range(2):
+                copy = sib_copy(g, kind, k)
+                copy.start()
+                across.append(copy)
+        if g == 0:
+            each(NDOM, make_slots)
+            sums[32] = jnp.zeros((144, 128), F32)
+            same = lax.broadcasted_iota(jnp.int32, (16, 16), 0) == lax.broadcasted_iota(
+                jnp.int32, (16, 16), 1
+            )
+            gain = jnp.zeros((16, 128), F32)
+            for s in range(4):
+                column = jnp.sum(jnp.where(same, gain_ref[s : s + 1, :], 0.0), axis=1, keepdims=True)
+                gain = gain + jnp.where(spec_ref[...] == s, column, 0.0)
     for copy in env_copies:
         copy.wait_recv()
     last = remote(ge.at[core], ge.at[core], own_send.at[2], own_recv.at[2], dom, sib)
     last.start()
     across.append(last)
+    each(15, lambda q: lat_copy(q).wait_recv())
+    for n in range(4):
+        block = x_in[4 * n : 4 * n + 4].reshape(256, 256).astype(F32)
+        x_t[:, 256 * n : 256 * n + 256] = block.T.astype(BF16)
     for g in range(2):
-        for i, k in enumerate((2, 1, 3)):
+        for half in range(2):
             for kind in range(2):
-                second[g][2 * i + kind].wait_recv()
-                copy = sib_copy(g, kind, k)
+                relays[g][kind, half].wait_recv()
+                copy = sib_copy(g, kind, 2, half)
                 copy.start()
                 across.append(copy)
-        if g == 0:
-            each(15, lambda q: lat_copy(q).wait_recv())
-            for n in range(4):
-                block = x_in[4 * n : 4 * n + 4].reshape(256, 256).astype(F32)
-                x_t[:, 256 * n : 256 * n + 256] = block.T.astype(BF16)
 
     def sib_arrivals(kind):
         own_copies[kind].wait_recv()
         for g in range(2):
-            for k in range(SIDE):
+            for k in (0, 1, 3):
                 sib_copy(g, kind, k).wait_recv()
+            for half in range(2):
+                sib_copy(g, kind, 2, half).wait_recv()
 
     sib_arrivals(0)
 
@@ -369,13 +393,8 @@
             )
             sums[2 * t + j] = dot(contrib, onehot[2 * t + j], ((1,), (1,)))
 
-    block_sums(me)
-
-    def arrived_sums(q):
-        w_copy(14 - q).wait_recv()
-        block_sums(tp_source(14 - q))
-
-    each(15, arrived_sums)
+    each(15, lambda q: w_copy(q).wait_recv())
+    each(NTP, block_sums, unroll=4)
 
     def domain_sum(d):
         total = sums[slots[4 * d]] + sums[slots[4 * d + 1]]
@@ -455,8 +474,11 @@
     each(15, lambda q: ln_copy(q).wait_recv())
     for copy in tile_copies + own_copies + first[0] + first[1] + env_copies:
         copy.wait_send()
-    for copy in second[0] + second[1] + across:
+    for copy in across:
         copy.wait_send()
+    for copies in second + relays:
+        for copy in copies.values():
+            copy.wait_send()
     for make in (lat_copy, w_copy, ln_copy):
         each(15, lambda q: make(q).wait_send())
     for part in range(2):
@@ -538,7 +560,7 @@
             dma((16,)),
             dma((15,)), dma((15,)), dma((15,)), dma((15,)), dma((3,)), dma((3,)),
             dma((2, 2, 4)), dma((2, 2, 4)), dma((2, 2, 4)), dma((2, 2, 4)), dma((4,)), dma((4,)),
-            dma((2, 2, 4)), dma((2, 2, 4)),
+            dma((2, 2, 5)), dma((2, 2, 5)),
             dma((15,)), dma((15,)), dma((15,)), dma((15,)),
             dma((2, 15)), dma((2, 15)), dma((2, 15)), dma((2, 15)),
         ],

time: 75 us -> 69.3 us (0.924)
  Pallas kernels: 73.6 us -> 68.5 us
    pallas_call x1, Pallas kernels: 71.4 us -> 66.3 us  [on_device(): pl.pallas_call(kernel, out_shape=shapes, in_specs=[hbm] * 10, out_specs=(...]
where the time goes in v4:
time: 69.3 us; the launch traced here: 69.1 us
  Pallas kernels  68.5 us (99%)
    pallas_call x1, Pallas kernels, on_device(): pl.pallas_call(kernel, out_shape=shapes, in_specs=[hbm] * 10, out_specs=(...  66.3 us
    pallas_call x1, Pallas kernels, on_device(): pl.pallas_call(write_out, out_shape=shapes, in_specs=[hbm] * 3, out_specs...  2.14 us

profile of v4, /device:TPU:8, one launch (start us, length us, event | category | flops | bytes accessed | tf_op | source)
XLA Modules:
  0.0 69.1 jit_solution(2335718413761891841)
XLA Ops:
  0.6 66.3 %allegro.1 = (bf16[64,4096]{1,0:T(8,128)(2,1)}, f32[9,16,128]{2,1,0:T(8,128)}, f32[3,16,4096]{2,1,0:T(8,128)}) custom-call(s32[32]{0:T(128)} %bitcast.6, s32[32]{0:T(128)} %fill.1, bf16[64,4096]{1,0:T(8,128)(2,1)} %latent.1, bf16[64,1024]{1,0:T(8,128)(2,1)} %bitcast.4, bf16[64,1024]{1,0:T(8,128)(2,1)} %w2.1, bf16[64,256]{1,0:T(8,128)(2,1)} %we.1, ...), custom_call_target="tpu_custom_call" | custom-call | flops 2000000000 | bytes 4000000 | tf_op jit(solution)/shard_map/allegro/pallas_call | solution.py:524
  67.0 2.1 %write_out.1 = (bf16[64,4096]{1,0:T(8,128)(2,1)}, f32[9,16,128]{2,1,0:T(8,128)}, f32[3,16,4096]{2,1,0:T(8,128)}) custom-call(bf16[64,4096]{1,0:T(8,128)(2,1)} %get-tuple-element.6.ln_in, f32[9,16,128]{2,1,0:T(8,128)} %get-tuple-element.7.env_in, f32[3,16,4096]{2,1,0:T(8,128)} %get-tuple-element.8.inv_in), custom_call_target="tpu_custom_call" | custom-call | tf_op jit(solution)/shard_map/write_out/pallas_call | solution.py:578

commit v5 on v4

--- a/solution.py
+++ b/solution.py
@@ -23,6 +23,7 @@
 DEPTH = 8
 HALF = DEPTH // 2
 NEAR_Z = (6, 2, 7, 1, 4, 5, 3)
+ENV_Z = (4, 5, 3, 6, 2, 7, 1)
 FAR = sorted(
     [(dx, dy) for dx in range(SIDE) for dy in range(SIDE) if dx or dy],
     key=lambda d: -min(d[0], SIDE - d[0]) - min(d[1], SIDE - d[1]),
@@ -86,6 +87,7 @@
         ),
         pltpu.make_async_copy(w1, own1.at[core], pre_sem.at[8]),
         pltpu.make_async_copy(w2, own2.at[core], pre_sem.at[9]),
+        pltpu.make_async_copy(we, ge.at[z, core], pre_sem.at[4]),
     ]
     for half in range(2):
         lanes = pl.ds(pl.multiple_of(by * 256 + 128 * half, 128), 128)
@@ -96,12 +98,6 @@
                     pieces.at[half, i], pre_sem.at[2 * i + half],
                 )
             )
-        pre.append(
-            pltpu.make_async_copy(
-                we.at[pl.ds((by, ax)[half] * 16, 16), pl.ds(128 * half, 128)],
-                pieces.at[half, 2], pre_sem.at[4 + half],
-            )
-        )
     for copy in pre:
         copy.start()
 
@@ -126,7 +122,6 @@
         pl.semaphore_signal(barrier, inc=1, device_id=(dom_far(q), me), device_id_type=MESH)
     for copy in pre:
         copy.wait()
-    ring[pl.ds(14 + core, 1)] = pieces[pl.ds(core, 1)]
     pl.semaphore_wait(barrier, NTP - 1 + NDOM - 1)
 
     def one_copy(n, c):
@@ -142,11 +137,6 @@
         ).wait_recv()
 
     tile_copies = [one_copy(n, c) for n in range(7) for c in range(2)]
-    tile_copies.append(
-        remote(
-            pieces.at[other], ring.at[14 + core], one_send.at[14], one_recv.at[14], dom, sib
-        )
-    )
     own_copies = [
         remote(ref.at[core], ref.at[core], own_send.at[i], own_recv.at[i], dom, sib)
         for i, ref in enumerate([own1, own2])
@@ -234,7 +224,6 @@
     first = []
     second = []
     across = []
-    env_row = by * other + ax * core
     env_copies = []
     for g in range(2):
         for slot in range(groups[g].start, groups[g].stop):
@@ -253,21 +242,12 @@
         first.append(copies)
         if g == 1:
             each(15, lambda q: lat_copy(q).start())
-            tile_copies[14].wait_recv()
             for n in range(7):
-                for c in range(2):
-                    chip = (z + DEPTH - NEAR_Z[n]) % DEPTH
-                    ge[pl.ds(core, 1), pl.ds(2 * chip + c, 1), pl.ds(env_row, 1)] = ring[
-                        2 * n + c, 2
-                    ][None, None, None]
-            for c in range(2):
-                ge[pl.ds(core, 1), pl.ds(2 * z + c, 1), pl.ds(env_row, 1)] = ring[14 + c, 2][
-                    None, None, None
-                ]
-            for k in (2, 1, 3):
-                three = ge.at[core, :, env_row]
-                to = (ax + k * core) % SIDE * SIDE + (by + k * other) % SIDE
-                env_copies.append(remote(three, three, e_send.at[k], e_recv.at[k], to, me))
+                mine = ge.at[z, core]
+                to = 2 * ((z + ENV_Z[n]) % DEPTH) + core
+                env_copies.append(
+                    remote(mine, mine, e_send.at[n], e_recv.at[n], dom, to)
+                )
             for copy in env_copies:
                 copy.start()
         for copy in copies:
@@ -323,11 +303,6 @@
             for s in range(4):
                 column = jnp.sum(jnp.where(same, gain_ref[s : s + 1, :], 0.0), axis=1, keepdims=True)
                 gain = gain + jnp.where(spec_ref[...] == s, column, 0.0)
-    for copy in env_copies:
-        copy.wait_recv()
-    last = remote(ge.at[core], ge.at[core], own_send.at[2], own_recv.at[2], dom, sib)
-    last.start()
-    across.append(last)
     each(15, lambda q: lat_copy(q).wait_recv())
     for n in range(4):
         block = x_in[4 * n : 4 * n + 4].reshape(256, 256).astype(F32)
@@ -340,6 +315,12 @@
                 copy.start()
                 across.append(copy)
 
+    for copy in env_copies:
+        copy.wait_recv()
+    last = remote(ge.at[:, core], ge.at[:, core], own_send.at[2], own_recv.at[2], dom, sib)
+    last.start()
+    across.append(last)
+
     def sib_arrivals(kind):
         own_copies[kind].wait_recv()
         for g in range(2):
@@ -372,8 +353,7 @@
         lnt[:, lanes] = (x_t[:, lanes].astype(F32) + update).astype(BF16)
 
     last.wait_recv()
-    matrix = jnp.concatenate([ge[c].reshape(1024, 128) for c in range(2)], axis=1)
-    env_weights = dot(lnt[...], matrix, ((1,), (0,)))
+    env_weights = dot(lnt[...], ge[...].reshape(1024, 256), ((1,), (0,)))
     ws[...] = env_weights.T.astype(BF16).reshape(16, 16, 256)
     each(15, lambda q: w_copy(q).start())
     wt[pl.ds(me, 1)] = ws[pl.ds(me, 1)]
@@ -427,6 +407,8 @@
     own.start()
     each(15, lambda q: ln_copy(q).start())
     total = domain_sum(dom)
+    in_low[pl.ds(dom, 1)] = jnp.zeros((1, 64, 128), BF16)
+    in_high[pl.ds(dom, 1)] = jnp.zeros((1, 80, 128), BF16)
     for part in range(2):
         into, ref = ((in_low, table_low), (in_high, table_high))[part]
         rows = (slice(0, 64), slice(64, 144))[part]
@@ -434,10 +416,9 @@
         for q in range(NDOM - 1):
             q_copy(part, q).wait_recv()
 
-        def add(k, acc):
-            return acc + into[(dom + k) % NDOM].astype(F32)
-
-        acc = lax.fori_loop(1, NDOM, add, total[rows])
+        acc = total[rows]
+        for d in range(NDOM):
+            acc = acc + into[d].astype(F32)
         env = acc.reshape(-1, 16, 128) * gain[None] * env_factor
         ref[pl.ds(dom, 1)] = env.reshape(1, -1, 128).astype(BF16)
         for q in range(NDOM - 1):
@@ -533,13 +514,13 @@
             pltpu.VMEM((32, 128), jnp.int32),
             pltpu.VMEM((1, 128), jnp.int32),
             pltpu.VMEM((4, 16), F32),
-            pltpu.VMEM((2, 3, 16, 128), BF16),
-            pltpu.VMEM((16, 3, 16, 128), BF16),
+            pltpu.VMEM((2, 2, 16, 128), BF16),
+            pltpu.VMEM((14, 2, 16, 128), BF16),
             pltpu.VMEM((2, 64, 1024), BF16),
             pltpu.VMEM((2, 64, 1024), BF16),
             pltpu.VMEM((2, 4, 4, 14, 16, 128), BF16),
             pltpu.VMEM((2, 4, 4, 14, 16, 128), BF16),
-            pltpu.VMEM((2, 16, 4, 16, 128), BF16),
+            pltpu.VMEM((8, 2, 64, 256), BF16),
             pltpu.VMEM((16, 64, 256), BF16),
             pltpu.VMEM((256, 1024), BF16),
             pltpu.VMEM((4, 256, 256), BF16),
@@ -559,7 +540,7 @@
             pltpu.VMEM((16, 80, 128), BF16),
             dma((16,)),
             dma((15,)), dma((15,)), dma((15,)), dma((15,)), dma((3,)), dma((3,)),
-            dma((2, 2, 4)), dma((2, 2, 4)), dma((2, 2, 4)), dma((2, 2, 4)), dma((4,)), dma((4,)),
+            dma((2, 2, 4)), dma((2, 2, 4)), dma((2, 2, 4)), dma((2, 2, 4)), dma((7,)), dma((7,)),
             dma((2, 2, 5)), dma((2, 2, 5)),
             dma((15,)), dma((15,)), dma((15,)), dma((15,)),
             dma((2, 15)), dma((2, 15)), dma((2, 15)), dma((2, 15)),

time: 69.3 us -> 72.3 us (1.043); the launches traced: 69.1 us -> 71.3 us
  Pallas kernels: 68.5 us -> 70.7 us
    pallas_call x1, Pallas kernels: 66.3 us -> 68.5 us  [on_device(): pl.pallas_call(kernel, out_shape=shapes, in_specs=[hbm] * 10, out_specs=(...]
where the time goes in v5:
time: 72.3 us; the launch traced here: 71.3 us
  Pallas kernels  70.7 us (98%)
    pallas_call x1, Pallas kernels, on_device(): pl.pallas_call(kernel, out_shape=shapes, in_specs=[hbm] * 10, out_specs=(...  68.5 us
    pallas_call x1, Pallas kernels, on_device(): pl.pallas_call(write_out, out_shape=shapes, in_specs=[hbm] * 3, out_specs...  2.14 us

profile of v5, /device:TPU:8, one launch (start us, length us, event | category | flops | bytes accessed | tf_op | source)
XLA Modules:
  0.0 71.3 jit_solution(4905493404908554534)
XLA Ops:
  0.6 68.5 %allegro.1 = (bf16[64,4096]{1,0:T(8,128)(2,1)}, f32[9,16,128]{2,1,0:T(8,128)}, f32[3,16,4096]{2,1,0:T(8,128)}) custom-call(s32[32]{0:T(128)} %bitcast.6, s32[32]{0:T(128)} %fill.1, bf16[64,4096]{1,0:T(8,128)(2,1)} %latent.1, bf16[64,1024]{1,0:T(8,128)(2,1)} %bitcast.4, bf16[64,1024]{1,0:T(8,128)(2,1)} %w2.1, bf16[64,256]{1,0:T(8,128)(2,1)} %we.1, ...), custom_call_target="tpu_custom_call" | custom-call | flops 2000000000 | bytes 4000000 | tf_op jit(solution)/shard_map/allegro/pallas_call | solution.py:505
  69.2 2.1 %write_out.1 = (bf16[64,4096]{1,0:T(8,128)(2,1)}, f32[9,16,128]{2,1,0:T(8,128)}, f32[3,16,4096]{2,1,0:T(8,128)}) custom-call(bf16[64,4096]{1,0:T(8,128)(2,1)} %get-tuple-element.6.ln_in, f32[9,16,128]{2,1,0:T(8,128)} %get-tuple-element.7.env_in, f32[3,16,4096]{2,1,0:T(8,128)} %get-tuple-element.8.inv_in), custom_call_target="tpu_custom_call" | custom-call | tf_op jit(solution)/shard_map/write_out/pallas_call | solution.py:559

commit v6 on v4

--- a/solution.py
+++ b/solution.py
@@ -37,7 +37,7 @@
     dest, fill, latent, w1, w2, we, ev, cen, spec, gains,
     ln_out, env_out, inv_out,
     dest_ref, fill_ref, ev_ref, cen_ref, spec_ref, gain_ref,
-    pieces, ring, own1, own2, g1, g2, ge, x_in, x_t, hid, lnt, ln, ws, wt, hs, onehot, slots,
+    pieces, ring, own1, own2, g1, g2, ge, x_in, x_t, hid, update, lnt, ln, ws, wt, hs, onehot, slots,
     sums, p_low, p_high, in_low, in_high, table_low, table_high,
     pre_sem, lat_send, lat_recv, one_send, one_recv, own_send, own_recv,
     a_send, a_recv, b_send, b_recv, e_send, e_recv,
@@ -332,7 +332,7 @@
     for n in range(4):
         block = x_in[4 * n : 4 * n + 4].reshape(256, 256).astype(F32)
         x_t[:, 256 * n : 256 * n + 256] = block.T.astype(BF16)
-    for g in range(2):
+    def pass_relays(g):
         for half in range(2):
             for kind in range(2):
                 relays[g][kind, half].wait_recv()
@@ -340,36 +340,60 @@
                 copy.start()
                 across.append(copy)
 
-    def sib_arrivals(kind):
-        own_copies[kind].wait_recv()
-        for g in range(2):
-            for k in (0, 1, 3):
-                sib_copy(g, kind, k).wait_recv()
-            for half in range(2):
-                sib_copy(g, kind, 2, half).wait_recv()
-
-    sib_arrivals(0)
-
-    def first_layer(r):
-        tiles = jnp.concatenate(
-            [g1[c, b, r].reshape(224, 128) for b in range(SIDE) for c in range(2)], axis=1
-        )
-        rows = pl.ds(pl.multiple_of(16 * r, 16), 16)
-        matrix = jnp.concatenate([tiles, own1[0, rows, :], own1[1, rows, :]], axis=0)
-        v = dot(x_t[...], matrix, ((1,), (1,)))
-        hid[r] = (v / (1.0 + jnp.exp(-v))).astype(BF16)
-
-    each(SIDE, first_layer)
-    sib_arrivals(1)
+    def sib_arrivals(g, kind):
+        for k in (0, 1, 3):
+            sib_copy(g, kind, k).wait_recv()
+        for half in range(2):
+            sib_copy(g, kind, 2, half).wait_recv()
+
+    def first_layer(g):
+        def layer(r):
+            rows = pl.ds(pl.multiple_of(16 * r, 16), 16)
+            tiles = jnp.concatenate(
+                [
+                    g1[c, b, r, groups[g]].reshape(-1, 128)
+                    for b in range(SIDE)
+                    for c in range(2)
+                ],
+                axis=1,
+            )
+            if g == 1:
+                tiles = jnp.concatenate([tiles, own1[0, rows, :], own1[1, rows, :]], axis=0)
+            v = dot(x_t[...], tiles, ((1,), (1,)))
+            hid[g, r] = (v / (1.0 + jnp.exp(-v))).astype(BF16)
+
+        each(SIDE, layer)
+
+    def second_layer(g, b):
+        lanes = slice(256 * b, 256 * b + 256)
+        matrix = []
+        for r in range(SIDE):
+            tiles = jnp.concatenate(
+                [g2[c, r, b, groups[g]].reshape(-1, 128) for c in range(2)], axis=1
+            )
+            matrix.append(tiles)
+            if g == 1:
+                rows = slice(16 * r, 16 * r + 16)
+                matrix += [own2[0, rows, lanes], own2[1, rows, lanes]]
+        hidden = jnp.concatenate([hid[g, r] for r in range(SIDE)], axis=1)
+        return dot(hidden, jnp.concatenate(matrix, axis=0), ((1,), (0,)))
+
+    pass_relays(0)
+    sib_arrivals(0, 0)
+    first_layer(0)
+    sib_arrivals(0, 1)
+    for b in range(SIDE):
+        update[:, 256 * b : 256 * b + 256] = second_layer(0, b)
+    pass_relays(1)
+    own_copies[0].wait_recv()
+    sib_arrivals(1, 0)
+    first_layer(1)
+    own_copies[1].wait_recv()
+    sib_arrivals(1, 1)
     for b in range(SIDE):
         lanes = slice(256 * b, 256 * b + 256)
-        update = jnp.zeros((256, 256), F32)
-        for r in range(SIDE):
-            tiles = jnp.concatenate([g2[c, r, b].reshape(224, 128) for c in range(2)], axis=1)
-            rows = slice(16 * r, 16 * r + 16)
-            matrix = jnp.concatenate([tiles, own2[0, rows, lanes], own2[1, rows, lanes]], axis=0)
-            update = update + dot(hid[r], matrix, ((1,), (0,)))
-        lnt[:, lanes] = (x_t[:, lanes].astype(F32) + update).astype(BF16)
+        total = update[:, lanes] + second_layer(1, b)
+        lnt[:, lanes] = (x_t[:, lanes].astype(F32) + total).astype(BF16)
 
     last.wait_recv()
     matrix = jnp.concatenate([ge[c].reshape(1024, 128) for c in range(2)], axis=1)
@@ -427,6 +451,8 @@
     own.start()
     each(15, lambda q: ln_copy(q).start())
     total = domain_sum(dom)
+    in_low[pl.ds(dom, 1)] = jnp.zeros((1, 64, 128), BF16)
+    in_high[pl.ds(dom, 1)] = jnp.zeros((1, 80, 128), BF16)
     for part in range(2):
         into, ref = ((in_low, table_low), (in_high, table_high))[part]
         rows = (slice(0, 64), slice(64, 144))[part]
@@ -434,10 +460,9 @@
         for q in range(NDOM - 1):
             q_copy(part, q).wait_recv()
 
-        def add(k, acc):
-            return acc + into[(dom + k) % NDOM].astype(F32)
-
-        acc = lax.fori_loop(1, NDOM, add, total[rows])
+        acc = total[rows]
+        for d in range(NDOM):
+            acc = acc + into[d].astype(F32)
         env = acc.reshape(-1, 16, 128) * gain[None] * env_factor
         ref[pl.ds(dom, 1)] = env.reshape(1, -1, 128).astype(BF16)
         for q in range(NDOM - 1):
@@ -542,7 +567,8 @@
             pltpu.VMEM((2, 16, 4, 16, 128), BF16),
             pltpu.VMEM((16, 64, 256), BF16),
             pltpu.VMEM((256, 1024), BF16),
-            pltpu.VMEM((4, 256, 256), BF16),
+            pltpu.VMEM((2, 4, 256, 128), BF16),
+            pltpu.VMEM((256, 1024), F32),
             pltpu.VMEM((256, 1024), BF16),
             pltpu.VMEM((16, 64, 256), BF16),
             pltpu.VMEM((16, 16, 256), BF16),

time: 69.3 us -> 70 us (1.010)
  no operation moved by 1% of the time
where the time goes in v6:
time: 70 us; the launch traced here: 69.6 us
  Pallas kernels  68.9 us (98%)
    pallas_call x1, Pallas kernels, on_device(): pl.pallas_call(kernel, out_shape=shapes, in_specs=[hbm] * 10, out_specs=(...  66.8 us
    pallas_call x1, Pallas kernels, on_device(): pl.pallas_call(write_out, out_shape=shapes, in_specs=[hbm] * 3, out_specs...  2.14 us

profile of v6, /device:TPU:8, one launch (start us, length us, event | category | flops | bytes accessed | tf_op | source)
XLA Modules:
  0.0 69.6 jit_solution(13425587584891874)
XLA Ops:
  0.6 66.8 %allegro.1 = (bf16[64,4096]{1,0:T(8,128)(2,1)}, f32[9,16,128]{2,1,0:T(8,128)}, f32[3,16,4096]{2,1,0:T(8,128)}) custom-call(s32[32]{0:T(128)} %bitcast.6, s32[32]{0:T(128)} %fill.1, bf16[64,4096]{1,0:T(8,128)(2,1)} %latent.1, bf16[64,1024]{1,0:T(8,128)(2,1)} %bitcast.4, bf16[64,1024]{1,0:T(8,128)(2,1)} %w2.1, bf16[64,256]{1,0:T(8,128)(2,1)} %we.1, ...), custom_call_target="tpu_custom_call" | custom-call | flops 2000000000 | bytes 4000000 | tf_op jit(solution)/shard_map/allegro/pallas_call | solution.py:549
  67.4 2.1 %write_out.1 = (bf16[64,4096]{1,0:T(8,128)(2,1)}, f32[9,16,128]{2,1,0:T(8,128)}, f32[3,16,4096]{2,1,0:T(8,128)}) custom-call(bf16[64,4096]{1,0:T(8,128)(2,1)} %get-tuple-element.6.ln_in, f32[9,16,128]{2,1,0:T(8,128)} %get-tuple-element.7.env_in, f32[3,16,4096]{2,1,0:T(8,128)} %get-tuple-element.8.inv_in), custom_call_target="tpu_custom_call" | custom-call | tf_op jit(solution)/shard_map/write_out/pallas_call | solution.py:604

commit v7 on v4

--- a/solution.py
+++ b/solution.py
@@ -251,8 +251,9 @@
         for copy in copies:
             copy.start()
         first.append(copies)
+        if g == 0:
+            each(15, lambda q: lat_copy(q).start())
         if g == 1:
-            each(15, lambda q: lat_copy(q).start())
             tile_copies[14].wait_recv()
             for n in range(7):
                 for c in range(2):
@@ -427,6 +428,8 @@
     own.start()
     each(15, lambda q: ln_copy(q).start())
     total = domain_sum(dom)
+    in_low[pl.ds(dom, 1)] = jnp.zeros((1, 64, 128), BF16)
+    in_high[pl.ds(dom, 1)] = jnp.zeros((1, 80, 128), BF16)
     for part in range(2):
         into, ref = ((in_low, table_low), (in_high, table_high))[part]
         rows = (slice(0, 64), slice(64, 144))[part]
@@ -434,10 +437,9 @@
         for q in range(NDOM - 1):
             q_copy(part, q).wait_recv()
 
-        def add(k, acc):
-            return acc + into[(dom + k) % NDOM].astype(F32)
-
-        acc = lax.fori_loop(1, NDOM, add, total[rows])
+        acc = total[rows]
+        for d in range(NDOM):
+            acc = acc + into[d].astype(F32)
         env = acc.reshape(-1, 16, 128) * gain[None] * env_factor
         ref[pl.ds(dom, 1)] = env.reshape(1, -1, 128).astype(BF16)
         for q in range(NDOM - 1):

time: 69.3 us -> 68.9 us (level)
  Pallas kernels: 68.5 us -> 67.7 us
    pallas_call x1, Pallas kernels: 66.3 us -> 65.6 us  [on_device(): pl.pallas_call(kernel, out_shape=shapes, in_specs=[hbm] * 10, out_specs=(...]
where the time goes in v7:
time: 68.9 us; the launch traced here: 68.4 us
  Pallas kernels  67.7 us (98%)
    pallas_call x1, Pallas kernels, on_device(): pl.pallas_call(kernel, out_shape=shapes, in_specs=[hbm] * 10, out_specs=(...  65.6 us
    pallas_call x1, Pallas kernels, on_device(): pl.pallas_call(write_out, out_shape=shapes, in_specs=[hbm] * 3, out_specs...  2.14 us

profile of v7, /device:TPU:8, one launch (start us, length us, event | category | flops | bytes accessed | tf_op | source)
XLA Modules:
  0.0 68.4 jit_solution(11885289768221987747)
XLA Ops:
  0.6 65.6 %allegro.1 = (bf16[64,4096]{1,0:T(8,128)(2,1)}, f32[9,16,128]{2,1,0:T(8,128)}, f32[3,16,4096]{2,1,0:T(8,128)}) custom-call(s32[32]{0:T(128)} %bitcast.6, s32[32]{0:T(128)} %fill.1, bf16[64,4096]{1,0:T(8,128)(2,1)} %latent.1, bf16[64,1024]{1,0:T(8,128)(2,1)} %bitcast.4, bf16[64,1024]{1,0:T(8,128)(2,1)} %w2.1, bf16[64,256]{1,0:T(8,128)(2,1)} %we.1, ...), custom_call_target="tpu_custom_call" | custom-call | flops 2000000000 | bytes 4000000 | tf_op jit(solution)/shard_map/allegro/pallas_call | solution.py:526
  66.2 2.1 %write_out.1 = (bf16[64,4096]{1,0:T(8,128)(2,1)}, f32[9,16,128]{2,1,0:T(8,128)}, f32[3,16,4096]{2,1,0:T(8,128)}) custom-call(bf16[64,4096]{1,0:T(8,128)(2,1)} %get-tuple-element.6.ln_in, f32[9,16,128]{2,1,0:T(8,128)} %get-tuple-element.7.env_in, f32[3,16,4096]{2,1,0:T(8,128)} %get-tuple-element.8.inv_in), custom_call_target="tpu_custom_call" | custom-call | tf_op jit(solution)/shard_map/write_out/pallas_call | solution.py:580

commit v8 on v7

--- a/solution.py
+++ b/solution.py
@@ -395,7 +395,7 @@
             sums[2 * t + j] = dot(contrib, onehot[2 * t + j], ((1,), (1,)))
 
     each(15, lambda q: w_copy(q).wait_recv())
-    each(NTP, block_sums, unroll=4)
+    each(NTP, block_sums, unroll=8)
 
     def domain_sum(d):
         total = sums[slots[4 * d]] + sums[slots[4 * d + 1]]
@@ -470,7 +470,7 @@
     for part in range(2):
         for q in range(NDOM - 1):
             t_copy(part, q).wait_recv()
-        each(NTP, lambda t: finish(t, part), unroll=4)
+        each(NTP, lambda t: finish(t, part), unroll=8)
 
     own.wait()
     each(15, lambda q: ln_copy(q).wait_recv())

time: 68.9 us -> 68.3 us (level)
  no operation moved by 1% of the time
where the time goes in v8:
time: 68.3 us; the launch traced here: 67.7 us
  Pallas kernels  67.1 us (98%)
    pallas_call x1, Pallas kernels, on_device(): pl.pallas_call(kernel, out_shape=shapes, in_specs=[hbm] * 10, out_specs=(...  64.9 us
    pallas_call x1, Pallas kernels, on_device(): pl.pallas_call(write_out, out_shape=shapes, in_specs=[hbm] * 3, out_specs...  2.14 us

profile of v8, /device:TPU:8, one launch (start us, length us, event | category | flops | bytes accessed | tf_op | source)
XLA Modules:
  0.0 67.7 jit_solution(6308466332945737935)
XLA Ops:
  0.6 64.9 %allegro.1 = (bf16[64,4096]{1,0:T(8,128)(2,1)}, f32[9,16,128]{2,1,0:T(8,128)}, f32[3,16,4096]{2,1,0:T(8,128)}) custom-call(s32[32]{0:T(128)} %bitcast.6, s32[32]{0:T(128)} %fill.1, bf16[64,4096]{1,0:T(8,128)(2,1)} %latent.1, bf16[64,1024]{1,0:T(8,128)(2,1)} %bitcast.4, bf16[64,1024]{1,0:T(8,128)(2,1)} %w2.1, bf16[64,256]{1,0:T(8,128)(2,1)} %we.1, ...), custom_call_target="tpu_custom_call" | custom-call | flops 2000000000 | bytes 4000000 | tf_op jit(solution)/shard_map/allegro/pallas_call | solution.py:526
  65.6 2.1 %write_out.1 = (bf16[64,4096]{1,0:T(8,128)(2,1)}, f32[9,16,128]{2,1,0:T(8,128)}, f32[3,16,4096]{2,1,0:T(8,128)}) custom-call(bf16[64,4096]{1,0:T(8,128)(2,1)} %get-tuple-element.6.ln_in, f32[9,16,128]{2,1,0:T(8,128)} %get-tuple-element.7.env_in, f32[3,16,4096]{2,1,0:T(8,128)} %get-tuple-element.8.inv_in), custom_call_target="tpu_custom_call" | custom-call | tf_op jit(solution)/shard_map/write_out/pallas_call | solution.py:580

commit v9 on v8

--- a/solution.py
+++ b/solution.py
@@ -121,7 +121,7 @@
     def greet_tp(q):
         pl.semaphore_signal(barrier, inc=1, device_id=(dom, tp_far(q)), device_id_type=MESH)
 
-    each(NTP - 1, greet_tp)
+    each(NTP - 1, greet_tp, unroll=NTP - 1)
     for q in range(NDOM - 1):
         pl.semaphore_signal(barrier, inc=1, device_id=(dom_far(q), me), device_id_type=MESH)
     for copy in pre:
@@ -376,7 +376,7 @@
     matrix = jnp.concatenate([ge[c].reshape(1024, 128) for c in range(2)], axis=1)
     env_weights = dot(lnt[...], matrix, ((1,), (0,)))
     ws[...] = env_weights.T.astype(BF16).reshape(16, 16, 256)
-    each(15, lambda q: w_copy(q).start())
+    each(15, lambda q: w_copy(q).start(), unroll=15)
     wt[pl.ds(me, 1)] = ws[pl.ds(me, 1)]
 
     for b in range(SIDE):
@@ -394,7 +394,7 @@
             )
             sums[2 * t + j] = dot(contrib, onehot[2 * t + j], ((1,), (1,)))
 
-    each(15, lambda q: w_copy(q).wait_recv())
+    each(15, lambda q: w_copy(q).wait_recv(), unroll=15)
     each(NTP, block_sums, unroll=8)
 
     def domain_sum(d):

time: 68.3 us -> 68.7 us (level)
  no operation moved by 1% of the time
where the time goes in v9:
time: 68.7 us; the launch traced here: 67.5 us
  Pallas kernels  66.8 us (97%)
    pallas_call x1, Pallas kernels, on_device(): pl.pallas_call(kernel, out_shape=shapes, in_specs=[hbm] * 10, out_specs=(...  64.7 us
    pallas_call x1, Pallas kernels, on_device(): pl.pallas_call(write_out, out_shape=shapes, in_specs=[hbm] * 3, out_specs...  2.14 us

profile of v9, /device:TPU:8, one launch (start us, length us, event | category | flops | bytes accessed | tf_op | source)
XLA Modules:
  0.0 67.5 jit_solution(14027562621010922264)
XLA Ops:
  0.6 64.7 %allegro.1 = (bf16[64,4096]{1,0:T(8,128)(2,1)}, f32[9,16,128]{2,1,0:T(8,128)}, f32[3,16,4096]{2,1,0:T(8,128)}) custom-call(s32[32]{0:T(128)} %bitcast.6, s32[32]{0:T(128)} %fill.1, bf16[64,4096]{1,0:T(8,128)(2,1)} %latent.1, bf16[64,1024]{1,0:T(8,128)(2,1)} %bitcast.4, bf16[64,1024]{1,0:T(8,128)(2,1)} %w2.1, bf16[64,256]{1,0:T(8,128)(2,1)} %we.1, ...), custom_call_target="tpu_custom_call" | custom-call | flops 2000000000 | bytes 4000000 | tf_op jit(solution)/shard_map/allegro/pallas_call | solution.py:526
  65.3 2.1 %write_out.1 = (bf16[64,4096]{1,0:T(8,128)(2,1)}, f32[9,16,128]{2,1,0:T(8,128)}, f32[3,16,4096]{2,1,0:T(8,128)}) custom-call(bf16[64,4096]{1,0:T(8,128)(2,1)} %get-tuple-element.6.ln_in, f32[9,16,128]{2,1,0:T(8,128)} %get-tuple-element.7.env_in, f32[3,16,4096]{2,1,0:T(8,128)} %get-tuple-element.8.inv_in), custom_call_target="tpu_custom_call" | custom-call | tf_op jit(solution)/shard_map/write_out/pallas_call | solution.py:580
